TPU v7x, 256 devices: a whole 4x4x8 slice. The times are simulated.
256 devices in a mesh: ty: 8 (over z_hi, x), tx: 16 (over z_lo, y), ens: 2 (over core).
Axes of the slice: x: 4, y: 4, z: 8 (z_hi: 2, z_lo: 4; z = z_hi * 4 + z_lo), core: 2. Of those that a mesh axis runs over, the one named last changes fastest.
Arguments:
- anomalies: float32 [4, 8, 1024, 2048], P('ens', None, 'ty', 'tx'), may hold values from -6 to 6
- climate_variance: float32 [8, 1024, 2048], P(None, 'ty', 'tx'), may hold values from 0.05 to 2
Outputs:
- covaried: float32 [4, 8, 1024, 2048], P('ens', None, 'ty', 'tx')
All inputs are finite; a program needn't handle non-finite values.
Results may differ from a plain program's by a relative error of at most 0.0001.
Values sent between devices are 32-bit elements; how exact they have to be, the bound alone decides.
No kernel may reach another device: no remote copies, remote signals or barrier semaphores. Data moves between devices by JAX's collectives and lax.ppermute only.
A program may use at most 64 MiB of HBM per device.

v0:
```python
import functools
import math

import jax
import jax.numpy as jnp
import ml_dtypes
import numpy as np
from jax import lax
from jax.experimental import pallas as pl
from jax.experimental.pallas import tpu as pltpu
from jax.sharding import PartitionSpec as P

LEVELS = 5
N = 128
EXT = 24

root_three = math.sqrt(3.0)
norm_factor = 4.0 * math.sqrt(2.0)
low_taps = np.array([1.0 + root_three, 3.0 + root_three, 3.0 - root_three, 1.0 - root_three]) / norm_factor
high_taps = np.array([low_taps[3], -low_taps[2], low_taps[1], -low_taps[0]])


def express(rows, basis):
    solved = np.linalg.lstsq(basis.T, rows.T, rcond=1e-9)[0].T
    assert np.abs(solved @ basis - rows).max() < 1e-10
    return solved


def build():
    approx = np.zeros((N + 2, N))
    approx[2:] = np.eye(N)
    A = np.zeros((256, N))
    PM = np.zeros((256, N))
    level = np.zeros(256, int)
    is_low = np.zeros(256, bool)
    valid = np.zeros(256, bool)
    E = np.zeros((EXT, N))
    last = np.zeros((EXT, N))
    last_pm = np.zeros((EXT, N))
    ext_level = np.full(EXT, -1)
    ext_low = np.zeros(EXT, bool)
    S = np.zeros((LEVELS, N))
    T = []
    up = np.zeros((LEVELS, 3, N))
    down = np.zeros((LEVELS, 3, N))
    up_k = np.zeros((LEVELS, 4, 3))
    down_k = np.zeros((LEVELS, 4, 3))
    where_last = np.zeros((LEVELS, 4), int)
    offset, count = 0, N
    for l in range(LEVELS):
        half = count // 2
        bands = []
        for taps in (low_taps, high_taps):
            band = np.zeros((half + 2, N))
            for k in range(-2, half):
                for j in range(4):
                    if -2 <= 2 * k + j < count:
                        band[k + 2] += taps[j] * approx[2 * k + j + 2]
            bands.append(band)
        stride = 2**l
        for b, band in enumerate(bands):
            width = max(half, 8)
            start = offset + width - half
            A[start : start + half] = band[2:]
            valid[start : start + half] = True
            level[offset : offset + width] = l
            is_low[offset : offset + width] = b == 0
            for k in range(half):
                PM[start + k, 2 * stride * k + (0 if b == 0 else stride)] = 1.0
            for k in range(2):
                e = 4 * l + 2 * b + k
                where_last[l, 2 * b + k] = start + half - 2 + k
                ext_level[e], ext_low[e] = l, b == 0
                if l > 0 or k == 1:
                    E[e] = band[k]
                    last[e] = A[start + half - 2 + k]
                    last_pm[e] = PM[start + half - 2 + k]
                else:
                    ext_level[e] = -1
            offset += width
        S[l] = low_taps[2] * approx[2] + low_taps[3] * approx[3]
        t = low_taps[0] * approx[count] + low_taps[1] * approx[count + 1]
        if l == 0:
            T.append(t)
            up[0, 0], down[0, 0] = S[0], t
        else:
            if l == 1:
                T.append(t)
            T += [bands[0][half], bands[1][half]]
            up[l] = np.stack([approx[0], approx[1], S[l]])
            down[l] = np.stack([t, bands[0][half], bands[1][half]])
        up_k[l] = express(E[4 * l : 4 * l + 4], up[l])
        down_k[l] = express(last[4 * l : 4 * l + 4], down[l])
        approx, count = bands[0], half
    T = np.stack(T)
    same = (level[:, None] == level[None, :]) & valid[:, None] & valid[None, :]
    mask = same & ~(is_low[:, None] & is_low[None, :] & (level[:, None] < 4))
    c = {}
    c["A"], c["PM"] = A, PM
    c["E"] = E
    c["S"], c["T"] = S, T
    c["KE"], c["KA"] = express(E, S), express(last, T)
    place = np.zeros((256, EXT))
    for l in range(LEVELS):
        for q in range(4):
            place[where_last[l, q], 4 * l + q] = 1.0
    c["GS"] = (place @ c["KE"]).T
    columns = sorted({int(np.argmax(r)) for r in last_pm if r.any()})
    D = np.zeros((12, N))
    for i, col in enumerate(columns):
        D[i, col] = 1.0
    c["D"] = D
    c["KD"] = last_pm @ D.T
    Y = np.zeros((LEVELS, 8, N))
    PY = np.zeros((LEVELS, 8, N))
    PYC = np.zeros((LEVELS, 8, N))
    for l in range(LEVELS):
        if l == 0:
            Y[0, 3], Y[0, 7] = up[0, 0], down[0, 0]
            PY[0, 4:8] = last_pm[0:4]
        else:
            Y[l, 0:3], Y[l, 4:7] = up[l], down[l]
            PY[l, 0:4] = last_pm[4 * l : 4 * l + 4]
        PYC[l, 0:4] = last_pm[4 * l : 4 * l + 4]
    c["Y"], c["PY"], c["PYC"] = Y.reshape(40, N), PY.reshape(40, N), PYC.reshape(40, N)
    GK = np.zeros((256, 4))
    cup = np.zeros((4, 8, N))
    cdn = np.zeros((4, 8, N))
    hup = np.zeros((4, 8, 96))
    hdn = np.zeros((4, 8, 96))
    lane_level = level[128:]
    ext96 = np.tile(ext_level, 4)
    for l in range(LEVELS):
        for q in range(4):
            for j in range(3):
                row = 3 if l == 0 else j
                if l == 0 and j > 0:
                    continue
                GK[where_last[l, q], row] = up_k[l, q, j]
                if l == 0:
                    cup[3, 4 + q, :] = up_k[0, q, 0]
                    cdn[3, 4 + q, :] = down_k[0, q, 0]
                else:
                    cup[j, q, lane_level == l] = up_k[l, q, j]
                    cdn[j, q, lane_level == l] = down_k[l, q, j]
                hup[row, q, ext96 == l] = up_k[l, q, j]
                hdn[row, q, ext96 == l] = down_k[l, q, j]
    c["GK"] = GK
    c["cup"], c["cdn"], c["hup"], c["hdn"] = cup, cdn, hup, hdn
    c["m0"], c["m1"] = mask[:128, :128], mask[128:, 128:]
    ext_mask = (ext_level[:, None] == level[None, :]) & valid[None, :]
    ext_mask &= ~(ext_low[:, None] & is_low[None, :] & (level[None, :] < 4))
    c["mlh"] = ext_mask
    mth = np.zeros((8, N), bool)
    for q in range(4):
        low = q < 2
        mth[q] = valid[128:] & ~(low & is_low[128:] & (lane_level < 4))
        if q % 2 == 1:
            mth[4 + q] = ~(low & is_low[:128])
    c["mth"] = mth
    mch = np.zeros((8, EXT), bool)
    for q in range(4):
        low = q < 2
        mch[q] = (ext_level >= 0) & ~(low & ext_low & (ext_level < 4))
        mch[q] &= ~((ext_level == 0) & (q % 2 == 0))
    c["mch"] = np.tile(mch, (1, 4))
    c["lane_level"], c["ext_level"] = lane_level, ext_level
    return c


def three(matrix, axis, reverse=False):
    high = matrix.astype(ml_dtypes.bfloat16)
    low = (matrix - high.astype(np.float64)).astype(ml_dtypes.bfloat16)
    return np.concatenate([high, high, low], axis)


def pad_rows(matrix, rows):
    return np.concatenate([matrix, np.zeros((rows - matrix.shape[0], matrix.shape[1]))], 0)


def pad_cols(matrix, cols):
    return pad_rows(matrix.T, cols).T


@functools.cache
def constants():
    c = build()
    f32 = np.float32
    k = {}
    k["q_nt"] = three(np.concatenate([pad_rows(c["T"], 16), pad_rows(c["S"], 16)]), 1)
    k["d_nt"] = np.concatenate([pad_rows(c["D"], 16)] * 2, 1).astype(ml_dtypes.bfloat16)
    k["at"] = three(c["A"].T, 0)
    k["gs"] = three(pad_rows(c["GS"], 16), 0)
    k["e_nt"] = three(pad_rows(c["E"], 32), 1)
    k["ka"] = three(pad_rows(pad_cols(c["KA"], 16), 32), 1)
    k["kd"] = np.concatenate([pad_rows(pad_cols(c["KD"], 16), 32)] * 2, 1).astype(ml_dtypes.bfloat16)
    k["y0"] = three(pad_rows(c["Y"][:8], 16), 1)
    k["y1"] = three(c["Y"][8:], 1)
    k["y_nt"] = three(pad_rows(c["Y"], 48), 1)
    k["pt"] = np.concatenate([c["PM"].T] * 2, 0).astype(ml_dtypes.bfloat16)
    k["p0"] = np.concatenate([c["PM"][:128]] * 2, 1).astype(ml_dtypes.bfloat16)
    k["p1"] = np.concatenate([c["PM"][128:]] * 2, 1).astype(ml_dtypes.bfloat16)
    k["py0"] = np.concatenate([pad_rows(c["PY"][:8], 16)] * 2, 1).astype(ml_dtypes.bfloat16)
    k["py1"] = np.concatenate([c["PY"][8:]] * 2, 1).astype(ml_dtypes.bfloat16)
    k["pyc_nt"] = np.concatenate([pad_rows(c["PYC"], 48)] * 2, 1).astype(ml_dtypes.bfloat16)
    gk = pad_cols(c["GK"], 16)
    k["a0"] = np.concatenate([three(c["A"][:128], 1), three(gk[:128], 1)], 1)
    k["a1"] = np.concatenate([three(c["A"][128:], 1), three(gk[128:], 1)], 1)
    k["gkt"] = three(gk.T, 0)
    k["s0"] = three(c["A"][:128], 0)
    k["s1"] = three(c["A"][128:], 0)
    k["e_tn"] = three(pad_rows(c["E"], 32), 0)
    k["e4"] = three(np.concatenate([c["E"]] * 4), 0)
    ey = np.zeros((40, N))
    ey[4:8] = c["E"][0:4]
    for l in range(1, LEVELS):
        ey[8 * l : 8 * l + 4] = c["E"][4 * l : 4 * l + 4]
    k["o"] = three(np.concatenate([c["A"].T, ey.T, np.zeros((N, 24))], 1), 1)
    for name in ("cup", "cdn", "hup", "hdn"):
        k[name] = c[name].astype(f32)
    lane = c["lane_level"]
    k["fold"] = np.stack([np.broadcast_to(lane == l, (8, N)) for l in range(1, LEVELS)]).astype(f32)
    ext96 = np.tile(c["ext_level"], 4)
    k["foldx"] = np.stack([np.broadcast_to(ext96 == l, (8, 96)) for l in range(LEVELS)]).astype(f32)
    k["m0"], k["m1"] = c["m0"].astype(f32), c["m1"].astype(f32)
    k["mlh"], k["mth"], k["mch"] = c["mlh"].astype(f32), c["mth"].astype(f32), c["mch"].astype(f32)
    tl = np.zeros((LEVELS, 8, N))
    tl[0, 4:8] = 1.0
    for l in range(1, LEVELS):
        tl[l, 0:4, lane == l] = 1.0
    k["tl"] = tl.astype(f32)
    cl = np.zeros((LEVELS, 4, 8, 96))
    image = np.repeat(np.arange(4), EXT)
    for l in range(LEVELS):
        for i in range(4):
            rows = slice(4, 8) if l == 0 else slice(0, 4)
            cl[l, i, rows, (ext96 == l) & (image == i)] = 1.0
    k["cl"] = cl.astype(f32)
    return k


def split(x):
    high = x.astype(jnp.bfloat16).astype(jnp.float32)
    return high, x - high


def data3(x, axis):
    high, low = split(x)
    return jnp.concatenate([high, low, high], axis).astype(jnp.bfloat16)


def data2(x, axis):
    high, low = split(x)
    return jnp.concatenate([high, low], axis).astype(jnp.bfloat16)


def nn(a, b):
    return lax.dot_general(a, b, (((1,), (0,)), ((), ())), preferred_element_type=jnp.float32)


def nt(a, b):
    return lax.dot_general(a, b, (((1,), (1,)), ((), ())), preferred_element_type=jnp.float32)


def tn(a, b):
    return lax.dot_general(a, b, (((0,), (0,)), ((), ())), preferred_element_type=jnp.float32)


def lanes(x, i):
    return x[:, N * i : N * (i + 1)]


def rows(x, i):
    return x[N * i : N * (i + 1)]


def side_by_side(x):
    return jnp.concatenate([rows(x, i) for i in range(4)], 1)


def stacked(x):
    return jnp.concatenate([lanes(x, i) for i in range(4)], 0)


def zeros(*shape):
    return jnp.zeros(shape, jnp.float32)


def first_kernel(x_ref, clim_ref, q_nt, d_nt, a_ref, b_ref):
    even = lax.axis_index("tx") % 2 == 0
    ens = lax.axis_index("ens")
    x3 = data3(x_ref[...].reshape(4 * N, N), 1)
    u = nt(q_nt[...], x3)
    clim = clim_ref[ens]
    d = nt(d_nt[...], data2(clim, 1))
    right = [u[0:10, N * i : N * (i + 1)] for i in range(4)] + [d[0:12], zeros(4, N)]
    left = [u[16:26, N * i : N * (i + 1)] for i in range(4)] + [zeros(16, N)]
    right, left = jnp.concatenate(right, 0), jnp.concatenate(left, 0)
    a_ref[0] = jnp.where(even, right, left)
    b_ref[0] = jnp.where(even, left, right)


def columns_of(x3, from_right, k):
    fr = jnp.concatenate([from_right[10 * i : 10 * i + 5] for i in range(4)], 1)
    fr = jnp.concatenate([fr, zeros(11, 4 * N)], 0)
    return nn(x3, k["at"]) + tn(data3(fr, 0), k["gs"])


def left_columns(x3, from_left, k):
    fl = jnp.concatenate([from_left[10 * i : 10 * i + 10] for i in range(4)], 1)
    fl = jnp.concatenate([fl, zeros(6, 4 * N)], 0)
    zl = nt(k["e_nt"], x3) + nn(k["ka"], data3(fl, 0))
    return jnp.concatenate([zl[0:EXT, N * i : N * (i + 1)] for i in range(4)], 0)


def left_clim(from_left, k):
    d = jnp.concatenate([from_left[40:52], zeros(4, N)], 0)
    return nn(k["kd"], data2(d, 0))[0:EXT]


SECOND = ("at", "gs", "e_nt", "ka", "kd", "y0", "y1", "y_nt", "pt", "py0", "py1", "pyc_nt", "fold", "foldx")


def second_kernel(x_ref, clim_ref, ra_ref, rb_ref, *refs):
    k = {name: ref[...] for name, ref in zip(SECOND, refs)}
    a_ref, b_ref, up_ref = refs[len(SECOND) :]
    even = lax.axis_index("tx") % 2 == 0
    even_y = lax.axis_index("ty") % 2 == 0
    ens = lax.axis_index("ens")
    ra, rb = ra_ref[0], rb_ref[0]
    from_right, from_left = jnp.where(even, ra, rb), jnp.where(even, rb, ra)
    x3 = data3(x_ref[...].reshape(4 * N, N), 1)
    z = columns_of(x3, from_right, k)
    y0 = nn(k["y0"], data3(side_by_side(z[:, :N]), 0))[0:8]
    y1 = nn(k["y1"], data3(side_by_side(z[:, N:]), 0))
    strips = []
    for i in range(4):
        strip = lanes(y0, i)
        for l in range(4):
            strip = strip + k["fold"][l] * lanes(y1[8 * l : 8 * l + 8], i)
        strips.append(strip)
    zl = left_columns(x3, from_left, k)
    hy = nt(k["y_nt"], data3(zl, 1))
    corner = sum(k["foldx"][l] * hy[8 * l : 8 * l + 8] for l in range(LEVELS))
    clim = clim_ref[ens]
    cz = nn(data2(clim, 1), k["pt"])
    cy = nn(k["py0"], data2(cz[:, :N], 0))[0:8]
    cy1 = nn(k["py1"], data2(cz[:, N:], 0))
    for l in range(4):
        cy = cy + k["fold"][l] * cy1[8 * l : 8 * l + 8]
    cx = nt(k["pyc_nt"], data2(left_clim(from_left, k), 1))
    cc = sum(k["foldx"][l][:, :EXT] * cx[8 * l : 8 * l + 8] for l in range(LEVELS))
    up = [s[0:4] for s in strips] + [jnp.concatenate([corner[0:4], zeros(4, 32)], 1), zeros(12, N)]
    down = [s[4:8] for s in strips] + [jnp.concatenate([corner[4:8], cc[0:4], zeros(4, 8)], 1), zeros(4, N), cy]
    up, down = jnp.concatenate(up, 0), jnp.concatenate(down, 0)
    a_ref[0] = jnp.where(even_y, down, up)
    b_ref[0] = jnp.where(even_y, up, down)
    up_ref[0] = up


THIRD = (
    "at", "gs", "e_nt", "ka", "kd", "pt", "p0", "p1", "a0", "a1", "gkt", "s0", "s1", "e_tn", "e4",
    "o", "cup", "cdn", "hup", "hdn", "m0", "m1", "mlh", "mth", "mch", "tl", "cl",
)


def third_kernel(x_ref, xp_ref, clim_ref, ra_ref, rb_ref, rap_ref, rbp_ref, sa_ref, sb_ref, sap_ref, sbp_ref, up_ref, upp_ref, *refs):
    k = {name: ref[...] for name, ref in zip(THIRD, refs)}
    out_ref = refs[len(THIRD)]
    even = lax.axis_index("tx") % 2 == 0
    even_y = lax.axis_index("ty") % 2 == 0
    first = lax.axis_index("ens") == 0
    sides = []
    for x, ra, rb, sa, sb, up in (
        (x_ref, ra_ref, rb_ref, sa_ref, sb_ref, up_ref),
        (xp_ref, rap_ref, rbp_ref, sap_ref, sbp_ref, upp_ref),
    ):
        ra, rb, sa, sb, up = ra[0], rb[0], sa[0], sb[0], up[0]
        from_right, from_left = jnp.where(even, ra, rb), jnp.where(even, rb, ra)
        below, above = jnp.where(even_y, sa, sb), jnp.where(even_y, sb, sa)
        x3 = data3(x[...].reshape(4 * N, N), 1)
        z = columns_of(x3, from_right, k)
        u = jnp.concatenate([below[4 * i : 4 * i + 4] for i in range(4)], 1)
        u3 = data3(jnp.concatenate([u, zeros(12, 4 * N)], 0), 0)
        w0 = nn(k["a0"], jnp.concatenate([data3(side_by_side(z[:, :N]), 0), u3], 0))
        w1 = nn(k["a1"], jnp.concatenate([data3(side_by_side(z[:, N:]), 0), u3], 0))
        zl = left_columns(x3, from_left, k)
        hb = jnp.concatenate([below[16:20, 0:96], zeros(12, 96)], 0)
        lh = nn(data3(zl, 1), k["at"]) + tn(data3(hb, 0), k["gkt"])
        th = []
        for i in range(4):
            t = zeros(8, N)
            for j in range(4):
                t = t + k["cup"][j] * up[4 * i + j : 4 * i + j + 1] + k["cdn"][j] * above[4 * i + j : 4 * i + j + 1]
            th.append(t)
        ch = zeros(8, 96)
        for j in range(4):
            ch = ch + k["hup"][j] * up[16 + j : 17 + j, 0:96] + k["hdn"][j] * above[16 + j : 17 + j, 0:96]
        sides.append((w0, w1, lh, th, ch, from_left, above))
    own, other = sides
    cz = nn(data2(clim_ref[...].reshape(2 * N, N), 1), k["pt"])
    cz0 = jnp.concatenate([cz[:N, :N], cz[N:, :N]], 1)
    cz1 = jnp.concatenate([cz[:N, N:], cz[N:, N:]], 1)
    cw0 = nn(k["p0"], data2(cz0, 0))
    cw1 = nn(k["p1"], data2(cz1, 0))
    halo_left = [jnp.where(first, own[5], other[5]), jnp.where(first, other[5], own[5])]
    halo_above = [jnp.where(first, own[6], other[6]), jnp.where(first, other[6], own[6])]
    s0, s1, slh, sth = [None] * 4, [None] * 4, [None] * 4, [None] * 4
    vch = []
    for v in range(2):
        def variance(clim, mask, parts):
            total = parts[0] * parts[0]
            for part in parts[1:]:
                total = total + part * part
            return mask * (0.5 * clim + 0.125 * total)

        images = (v, v + 2)
        sides4 = [(side, i) for side in (own, other) for i in images]
        v0 = variance(lanes(cw0, v), k["m0"], [lanes(s[0], i) for s, i in sides4])
        v1 = variance(lanes(cw1, v), k["m1"], [lanes(s[1], i) for s, i in sides4])
        clh = nn(data2(left_clim(halo_left[v], k), 1), k["pt"])
        vlh = variance(clh, k["mlh"], [s[2][EXT * i : EXT * (i + 1)] for s, i in sides4])
        vth = variance(halo_above[v][24:32], k["mth"], [s[3][i] for s, i in sides4])
        cch = jnp.concatenate([halo_above[v][16:20, 96:120], zeros(4, EXT)], 0)
        vch.append(variance(cch, k["mch"][:, :EXT], [s[4][:, EXT * i : EXT * (i + 1)] for s, i in sides4]))
        for i in images:
            s0[i] = lanes(own[0], i) * v0
            s1[i] = lanes(own[1], i) * v1
            slh[i] = own[2][EXT * i : EXT * (i + 1)] * vlh
            sth[i] = own[3][i] * vth
    sch = own[4] * jnp.concatenate(vch + vch, 1)
    sch = jnp.concatenate([sch[0:4], sch[0:4]], 0)
    r0 = nn(data3(jnp.concatenate(s0, 0), 1), k["s0"])
    r1 = nn(data3(jnp.concatenate(s1, 0), 1), k["s1"])
    top0 = jnp.concatenate([k["tl"][0] * sth[i] for i in range(4)], 0)
    top1 = jnp.concatenate([k["tl"][l] * sth[i] for l in range(1, LEVELS) for i in range(4)], 0)
    corner = jnp.concatenate([k["cl"][l, i] * sch for l in range(LEVELS) for i in range(4)], 0)
    tu = jnp.concatenate([nn(data3(top0, 1), k["s0"]), nn(data3(top1, 1), k["s1"])], 0)
    tu = tu + nn(data3(corner, 1), k["e4"])
    full = []
    for i in range(4):
        r = tn(data3(jnp.concatenate([slh[i], zeros(8, 256)], 0), 0), k["e_tn"])
        t = jnp.concatenate([tu[8 * (4 * l + i) : 8 * (4 * l + i) + 8] for l in range(LEVELS)] + [zeros(24, N)], 0)
        full.append(jnp.concatenate([r[:N] + rows(r0, i), r[N:] + rows(r1, i), t], 0))
    out = nn(k["o"], data3(jnp.concatenate(full, 1), 0))
    for i in range(4):
        out_ref[i // 2, i % 2] = lanes(out, i)


def whole(array):
    zero = (0,) * array.ndim
    return pl.BlockSpec(array.shape, lambda p: zero)


def block(*shape):
    return pl.BlockSpec((1,) + shape, lambda p: (p, 0, 0))


def call(kernel, names, arguments, in_specs, out_specs, out_shape):
    consts = [jnp.asarray(constants()[name]) for name in names]
    return pl.pallas_call(
        kernel,
        grid=(4,),
        in_specs=in_specs + [whole(c) for c in consts],
        out_specs=out_specs,
        out_shape=out_shape,
        compiler_params=pltpu.CompilerParams(vmem_limit_bytes=48 * 1024 * 1024),
    )(*arguments, *consts)


def exchange(value, axis, odd):
    count = lax.axis_size(axis)
    pairs = [(i, (i + 1 if i % 2 == odd else i - 1) % count) for i in range(count)]
    return lax.ppermute(value, axis, pairs)


def partner(value):
    return lax.ppermute(value, "ens", [(0, 1), (1, 0)])


X_SPEC = pl.BlockSpec((2, 2, N, N), lambda p: (0, p, 0, 0))
CLIM_SPEC = pl.BlockSpec((2, N, N), lambda p: (p, 0, 0))


def shards(x, clim):
    xp = partner(x)
    m1 = jax.ShapeDtypeStruct((4, 56, N), jnp.float32)
    m2 = jax.ShapeDtypeStruct((4, 32, N), jnp.float32)
    b1, b2 = block(56, N), block(32, N)
    xa, xb = call(first_kernel, ("q_nt", "d_nt"), (x, clim), [X_SPEC, CLIM_SPEC], [b1, b1], [m1, m1])
    ra, rb = exchange(xa, "tx", 0), exchange(xb, "tx", 1)
    rap, rbp = partner(ra), partner(rb)
    ya, yb, up = call(second_kernel, SECOND, (x, clim, ra, rb), [X_SPEC, CLIM_SPEC, b1, b1], [b2, b2, b2], [m2, m2, m2])
    sa, sb = exchange(ya, "ty", 0), exchange(yb, "ty", 1)
    upp = partner(up)
    sap, sbp = partner(sa), partner(sb)
    return call(
        third_kernel,
        THIRD,
        (x, xp, clim, ra, rb, rap, rbp, sa, sb, sap, sbp, up, upp),
        [X_SPEC, X_SPEC, CLIM_SPEC] + [b1] * 4 + [b2] * 6,
        X_SPEC,
        jax.ShapeDtypeStruct(x.shape, jnp.float32),
    )


def solution(mesh):
    in_specs = (P("ens", None, "ty", "tx"), P(None, "ty", "tx"))
    out_specs = P("ens", None, "ty", "tx")
    return jax.shard_map(shards, mesh=mesh, in_specs=in_specs, out_specs=out_specs, check_vma=False)
```

profile of v0, /device:TPU:1, one launch (start us, length us, event | category | flops | bytes accessed | tf_op | source)
XLA Modules:
  0.0 52.4 jit_solution(9326437908517834521)
XLA Ops:
  0.0 3.2 %collective-permute-start = (f32[2,8,128,128]{3,2,1,0:T(8,128)}, f32[2,8,128,128]{3,2,1,0:T(8,128)S(1)}, u32[]{:S(2)}, u32[]{:S(2)}) collective-permute-start(f32[2,8,128,128]{3,2,1,0:T(8,128)} %x_ref.5), channel_id=1, source_target_pairs={{0,1},{1,0},{2,3},{3,2},{4,5},{5,4},{6,7},{7,6},{8,9},{9,8},{10,11... | collective-permute-start | bytes 3145736 | tf_op jit(solution)/shard_map/ppermute | solution.py:478
  3.3 1.2 %copy-done = f32[2,8,128,128]{3,2,1,0:T(8,128)S(1)} copy-done((f32[2,8,128,128]{3,2,1,0:T(8,128)S(1)}, f32[2,8,128,128]{3,2,1,0:T(8,128)}, u32[]{:S(2)}) %copy-start) | copy-done | bytes 1048600
  4.5 1.0 %copy-done.1 = f32[8,128,128]{2,1,0:T(8,128)S(1)} copy-done((f32[8,128,128]{2,1,0:T(8,128)S(1)}, f32[8,128,128]{2,1,0:T(8,128)}, u32[]{:S(2)}) %copy-start.1) | copy-done | bytes 524312
  5.5 0.0 copy-start.18
  5.6 0.0 copy-start.19
  5.6 0.0 copy-start.23
  5.6 0.0 copy-start.24
  5.6 0.0 copy-start.32
  5.6 0.0 copy-start.33
  5.6 0.0 copy-start.34
  5.6 0.0 copy-start.35
  5.7 1.2 %shard_map.361 = (f32[4,56,128]{2,1,0:T(8,128)S(1)}, f32[4,56,128]{2,1,0:T(8,128)S(1)}) custom-call(f32[2,8,128,128]{3,2,1,0:T(8,128)S(1)} %copy-done, f32[8,128,128]{2,1,0:T(8,128)S(1)} %copy-done.1, bf16[32,384]{1,0:T(8,128)(2,1)S(1)} %copy-done.25, bf16[16,256]{1,0:T(8,128)(2,1)S(1)} %copy-done.36), custom_call_target="tpu_custom_call" | custom-call | tf_op jit(solution)/shard_map/pallas_call | solution.py:461
  6.8 0.1 collective-permute-start.1
  6.9 0.0 copy-start.4
  7.0 0.0 copy-start.5
  7.0 0.0 copy-start.6
  7.0 0.0 copy-start.9
  7.0 0.0 copy-start.10
  7.0 0.0 copy-start.12
  7.0 0.0 copy-start.13
  7.0 0.0 copy-start.14
  7.1 5.6 %collective-permute-start.2 = (f32[4,56,128]{2,1,0:T(8,128)S(1)}, f32[4,56,128]{2,1,0:T(8,128)S(1)}, u32[]{:S(2)}, u32[]{:S(2)}) collective-permute-start(f32[4,56,128]{2,1,0:T(8,128)S(1)} %get-tuple-element.11), channel_id=1, source_target_pairs={{0,30},{2,4},{4,2},{6,8},{8,6},{10,12},{12,10},{14,16},{16,14},{18... | collective-permute-start | bytes 344072 | tf_op jit(solution)/shard_map/ppermute | solution.py:474
  12.7 2.5 %collective-permute-done.2.rb_ref = f32[4,56,128]{2,1,0:T(8,128)S(1)} collective-permute-done((f32[4,56,128]{2,1,0:T(8,128)S(1)}, f32[4,56,128]{2,1,0:T(8,128)S(1)}, u32[]{:S(2)}, u32[]{:S(2)}) %collective-permute-start.2) | collective-permute-done | bytes 114720 | tf_op jit(solution)/shard_map/ppermute | solution.py:474
  15.5 6.0 %shard_map.362 = (f32[4,32,128]{2,1,0:T(8,128)S(1)}, f32[4,32,128]{2,1,0:T(8,128)S(1)}, f32[4,32,128]{2,1,0:T(8,128)S(1)}) custom-call(f32[2,8,128,128]{3,2,1,0:T(8,128)S(1)} %copy-done, f32[8,128,128]{2,1,0:T(8,128)S(1)} %copy-done.1, f32[4,56,128]{2,1,0:T(8,128)S(1)} %collective-permute-done.1.ra_ref, f32[4,56,128]{2,1,0:T(8,128)S(1)} %collective-permute-done.2.rb_ref, ...), custom_call_target="tpu_custom_call" | custom-call | tf_op jit(solution)/shard_map/pallas_call | solution.py:461
  21.5 1.3 %collective-permute-start.5 = (f32[4,32,128]{2,1,0:T(8,128)S(1)}, f32[4,32,128]{2,1,0:T(8,128)S(1)}, u32[]{:S(2)}, u32[]{:S(2)}) collective-permute-start(f32[4,32,128]{2,1,0:T(8,128)S(1)} %get-tuple-element.12), channel_id=1, source_target_pairs={{0,32},{32,0},{64,96},{96,64},{128,160},{160,128},{192,224},{224,1... | collective-permute-start | bytes 196616 | tf_op jit(solution)/shard_map/ppermute | solution.py:474
  22.8 7.5 %collective-permute-start.6 = (f32[4,32,128]{2,1,0:T(8,128)S(1)}, f32[4,32,128]{2,1,0:T(8,128)S(1)}, u32[]{:S(2)}, u32[]{:S(2)}) collective-permute-start(f32[4,32,128]{2,1,0:T(8,128)S(1)} %get-tuple-element.13), channel_id=1, source_target_pairs={{0,224},{32,64},{64,32},{96,128},{128,96},{160,192},{192,160},{224... | collective-permute-start | bytes 196616 | tf_op jit(solution)/shard_map/ppermute | solution.py:474
  30.2 2.7 %collective-permute-start.9 = (f32[4,32,128]{2,1,0:T(8,128)S(1)}, f32[4,32,128]{2,1,0:T(8,128)S(1)}, u32[]{:S(2)}, u32[]{:S(2)}) collective-permute-start(f32[4,32,128]{2,1,0:T(8,128)S(1)} %get-tuple-element.14.up_ref), channel_id=1, source_target_pairs={{0,1},{1,0},{2,3},{3,2},{4,5},{5,4},{6,7},{7,6},{8,9},{9,8},{10,11... | collective-permute-start | bytes 196616 | tf_op jit(solution)/shard_map/ppermute | solution.py:478
  32.9 0.5 collective-permute-start.4
  33.4 2.4 %collective-permute-start.7 = (f32[4,32,128]{2,1,0:T(8,128)S(1)}, f32[4,32,128]{2,1,0:T(8,128)S(1)}, u32[]{:S(2)}, u32[]{:S(2)}) collective-permute-start(f32[4,32,128]{2,1,0:T(8,128)S(1)} %collective-permute-done.5.sa_ref), channel_id=1, source_target_pairs={{0,1},{1,0},{2,3},{3,2},{4,5},{5,4},{6,7},{7,6},{8,9},{9,8},{10,11... | collective-permute-start | bytes 196616 | tf_op jit(solution)/shard_map/ppermute | solution.py:478
  35.9 0.9 %collective-permute-done.7.sap_ref = f32[4,32,128]{2,1,0:T(8,128)S(1)} collective-permute-done((f32[4,32,128]{2,1,0:T(8,128)S(1)}, f32[4,32,128]{2,1,0:T(8,128)S(1)}, u32[]{:S(2)}, u32[]{:S(2)}) %collective-permute-start.7) | collective-permute-done | bytes 65568 | tf_op jit(solution)/shard_map/ppermute | solution.py:478
  36.8 0.4 collective-permute-done.8.sbp_ref
  37.3 15.1 %shard_map.363 = f32[2,8,128,128]{3,2,1,0:T(8,128)} custom-call(f32[2,8,128,128]{3,2,1,0:T(8,128)S(1)} %copy-done, f32[2,8,128,128]{3,2,1,0:T(8,128)S(1)} %collective-permute-done.xp_ref, f32[8,128,128]{2,1,0:T(8,128)S(1)} %copy-done.1, f32[4,56,128]{2,1,0:T(8,128)S(1)} %collective-permute-done.1.ra_ref, f32[4,56,128]{2,1,0:T(8,128)S(1)} %collective-permute-done.2.rb_ref, ...), custom_call_target="tpu_custom_call" | custom-call | tf_op jit(solution)/shard_map/pallas_call | solution.py:461
  (69 shorter events, 0.2 us)
Async XLA Ops:
  0.0 37.1 %collective-permute-start = (f32[2,8,128,128]{3,2,1,0:T(8,128)}, f32[2,8,128,128]{3,2,1,0:T(8,128)S(1)}, u32[]{:S(2)}, u32[]{:S(2)}) collective-permute-start(f32[2,8,128,128]{3,2,1,0:T(8,128)} %x_ref.5), channel_id=1, source_target_pairs={{0,1},{1,0},{2,3},{3,2},{4,5},{5,4},{6,7},{7,6},{8,9},{9,8},{10,11... | collective-permute-start | bytes 3145736 | tf_op jit(solution)/shard_map/ppermute | solution.py:478
  5.5 9.8 %copy-start.17 = (bf16[48,384]{1,0:T(8,128)(2,1)S(1)}, bf16[48,384]{1,0:T(8,128)(2,1)}, u32[]{:S(2)}) copy-start(bf16[48,384]{1,0:T(8,128)(2,1)} %constant.83.clone.refs_7_) | copy-start | bytes 110596
  6.8 5.9 %collective-permute-start.1 = (f32[4,56,128]{2,1,0:T(8,128)S(1)}, f32[4,56,128]{2,1,0:T(8,128)S(1)}, u32[]{:S(2)}, u32[]{:S(2)}) collective-permute-start(f32[4,56,128]{2,1,0:T(8,128)S(1)} %get-tuple-element.10), channel_id=1, source_target_pairs={{0,2},{2,0},{4,6},{6,4},{8,10},{10,8},{12,14},{14,12},{16,18},{18,... | collective-permute-start | bytes 344072 | tf_op jit(solution)/shard_map/ppermute | solution.py:474
  6.9 30.2 %copy-start.4 = (bf16[128,960]{1,0:T(8,128)(2,1)S(1)}, bf16[128,960]{1,0:T(8,128)(2,1)}, u32[]{:S(2)}) copy-start(bf16[128,960]{1,0:T(8,128)(2,1)} %constant.99.clone.refs_15_) | copy-start | bytes 737284
  7.0 30.2 %copy-start.5 = (bf16[128,432]{1,0:T(8,128)(2,1)S(1)}, bf16[128,432]{1,0:T(8,128)(2,1)}, u32[]{:S(2)}) copy-start(bf16[128,432]{1,0:T(8,128)(2,1)} %constant.93.clone.refs_9_) | copy-start | bytes 331780
  7.0 30.2 %copy-start.6 = (bf16[128,432]{1,0:T(8,128)(2,1)S(1)}, bf16[128,432]{1,0:T(8,128)(2,1)}, u32[]{:S(2)}) copy-start(bf16[128,432]{1,0:T(8,128)(2,1)} %constant.92.clone.refs_8_) | copy-start | bytes 331780
  7.0 30.2 %copy-start.9 = (bf16[384,128]{1,0:T(8,128)(2,1)S(1)}, bf16[384,128]{1,0:T(8,128)(2,1)}, u32[]{:S(2)}) copy-start(bf16[384,128]{1,0:T(8,128)(2,1)} %constant.96.clone.refs_12_) | copy-start | bytes 294916
  7.0 30.2 %copy-start.10 = (bf16[384,128]{1,0:T(8,128)(2,1)S(1)}, bf16[384,128]{1,0:T(8,128)(2,1)}, u32[]{:S(2)}) copy-start(bf16[384,128]{1,0:T(8,128)(2,1)} %constant.95.clone.refs_11_) | copy-start | bytes 294916
  7.0 30.2 %copy-start.11 = (f32[5,4,8,96]{3,2,1,0:T(8,128)S(1)}, f32[5,4,8,96]{3,2,1,0:T(8,128)}, u32[]{:S(2)}) copy-start(f32[5,4,8,96]{3,2,1,0:T(8,128)} %constant.110.clone.refs_26_) | copy-start | bytes 184324
  7.0 30.2 %copy-start.12 = (bf16[288,128]{1,0:T(8,128)(2,1)S(1)}, bf16[288,128]{1,0:T(8,128)(2,1)}, u32[]{:S(2)}) copy-start(bf16[288,128]{1,0:T(8,128)(2,1)} %constant.98.clone.refs_14_) | copy-start | bytes 221188
  7.0 30.1 %copy-start.13 = (f32[128,128]{1,0:T(8,128)S(1)}, f32[128,128]{1,0:T(8,128)}, u32[]{:S(2)}) copy-start(f32[128,128]{1,0:T(8,128)} %constant.105.clone.refs_21_) | copy-start | bytes 196612
  7.0 30.1 %copy-start.14 = (f32[128,128]{1,0:T(8,128)S(1)}, f32[128,128]{1,0:T(8,128)}, u32[]{:S(2)}) copy-start(f32[128,128]{1,0:T(8,128)} %constant.104.clone.refs_20_) | copy-start | bytes 196612
  7.1 30.1 %copy-start.15 = (bf16[128,256]{1,0:T(8,128)(2,1)S(1)}, bf16[128,256]{1,0:T(8,128)(2,1)}, u32[]{:S(2)}) copy-start(bf16[128,256]{1,0:T(8,128)(2,1)} %constant.91.clone.refs_7_) | copy-start | bytes 196612
  7.1 30.1 %copy-start.16 = (bf16[128,256]{1,0:T(8,128)(2,1)S(1)}, bf16[128,256]{1,0:T(8,128)(2,1)}, u32[]{:S(2)}) copy-start(bf16[128,256]{1,0:T(8,128)(2,1)} %constant.90.clone.refs_6_) | copy-start | bytes 196612
  7.1 30.1 %copy-start.20 = (f32[24,256]{1,0:T(8,128)S(1)}, f32[24,256]{1,0:T(8,128)}, u32[]{:S(2)}) copy-start(f32[24,256]{1,0:T(8,128)} %constant.106.clone.refs_22_) | copy-start | bytes 73732
  7.1 30.1 %copy-start.21 = (bf16[96,128]{1,0:T(8,128)(2,1)S(1)}, bf16[96,128]{1,0:T(8,128)(2,1)}, u32[]{:S(2)}) copy-start(bf16[96,128]{1,0:T(8,128)(2,1)} %constant.97.clone.refs_13_) | copy-start | bytes 73732
  7.1 30.1 %copy-start.22 = (bf16[48,256]{1,0:T(8,128)(2,1)S(1)}, bf16[48,256]{1,0:T(8,128)(2,1)}, u32[]{:S(2)}) copy-start(bf16[48,256]{1,0:T(8,128)(2,1)} %constant.94.clone.refs_10_) | copy-start | bytes 73732
  7.1 30.1 %copy-start.27 = (f32[5,8,128]{2,1,0:T(8,128)S(1)}, f32[5,8,128]{2,1,0:T(8,128)}, u32[]{:S(2)}) copy-start(f32[5,8,128]{2,1,0:T(8,128)} %constant.109.clone.refs_25_) | copy-start | bytes 61444
  7.1 8.2 %collective-permute-start.2 = (f32[4,56,128]{2,1,0:T(8,128)S(1)}, f32[4,56,128]{2,1,0:T(8,128)S(1)}, u32[]{:S(2)}, u32[]{:S(2)}) collective-permute-start(f32[4,56,128]{2,1,0:T(8,128)S(1)} %get-tuple-element.11), channel_id=1, source_target_pairs={{0,30},{2,4},{4,2},{6,8},{8,6},{10,12},{12,10},{14,16},{16,14},{18... | collective-permute-start | bytes 344072 | tf_op jit(solution)/shard_map/ppermute | solution.py:474
  15.4 21.8 %copy-start.28 = (f32[4,8,96]{2,1,0:T(8,128)S(1)}, f32[4,8,96]{2,1,0:T(8,128)}, u32[]{:S(2)}) copy-start(f32[4,8,96]{2,1,0:T(8,128)} %constant.103.clone.refs_19_) | copy-start | bytes 36868
  15.4 21.8 %copy-start.29 = (f32[4,8,96]{2,1,0:T(8,128)S(1)}, f32[4,8,96]{2,1,0:T(8,128)}, u32[]{:S(2)}) copy-start(f32[4,8,96]{2,1,0:T(8,128)} %constant.102.clone.refs_18_) | copy-start | bytes 36868
  15.4 21.8 %copy-start.30 = (f32[4,8,128]{2,1,0:T(8,128)S(1)}, f32[4,8,128]{2,1,0:T(8,128)}, u32[]{:S(2)}) copy-start(f32[4,8,128]{2,1,0:T(8,128)} %constant.101.clone.refs_17_) | copy-start | bytes 49156
  15.4 21.8 %copy-start.31 = (f32[4,8,128]{2,1,0:T(8,128)S(1)}, f32[4,8,128]{2,1,0:T(8,128)}, u32[]{:S(2)}) copy-start(f32[4,8,128]{2,1,0:T(8,128)} %constant.100.clone.refs_16_) | copy-start | bytes 49156
  15.5 21.8 %copy-start.38 = (f32[8,128]{1,0:T(8,128)S(1)}, f32[8,128]{1,0:T(8,128)}, u32[]{:S(2)}) copy-start(f32[8,128]{1,0:T(8,128)} %constant.107.clone.refs_23_) | copy-start | bytes 12292
  21.5 15.8 %copy-start.37 = (f32[8,96]{1,0:T(8,128)S(1)}, f32[8,96]{1,0:T(8,128)}, u32[]{:S(2)}) copy-start(f32[8,96]{1,0:T(8,128)} %constant.108.clone.refs_24_) | copy-start | bytes 9220
  21.5 11.4 %collective-permute-start.5 = (f32[4,32,128]{2,1,0:T(8,128)S(1)}, f32[4,32,128]{2,1,0:T(8,128)S(1)}, u32[]{:S(2)}, u32[]{:S(2)}) collective-permute-start(f32[4,32,128]{2,1,0:T(8,128)S(1)} %get-tuple-element.12), channel_id=1, source_target_pairs={{0,32},{32,0},{64,96},{96,64},{128,160},{160,128},{192,224},{224,1... | collective-permute-start | bytes 196616 | tf_op jit(solution)/shard_map/ppermute | solution.py:474
  22.8 10.7 %collective-permute-start.6 = (f32[4,32,128]{2,1,0:T(8,128)S(1)}, f32[4,32,128]{2,1,0:T(8,128)S(1)}, u32[]{:S(2)}, u32[]{:S(2)}) collective-permute-start(f32[4,32,128]{2,1,0:T(8,128)S(1)} %get-tuple-element.13), channel_id=1, source_target_pairs={{0,224},{32,64},{64,32},{96,128},{128,96},{160,192},{192,160},{224... | collective-permute-start | bytes 196616 | tf_op jit(solution)/shard_map/ppermute | solution.py:474
  30.2 5.6 %collective-permute-start.9 = (f32[4,32,128]{2,1,0:T(8,128)S(1)}, f32[4,32,128]{2,1,0:T(8,128)S(1)}, u32[]{:S(2)}, u32[]{:S(2)}) collective-permute-start(f32[4,32,128]{2,1,0:T(8,128)S(1)} %get-tuple-element.14.up_ref), channel_id=1, source_target_pairs={{0,1},{1,0},{2,3},{3,2},{4,5},{5,4},{6,7},{7,6},{8,9},{9,8},{10,11... | collective-permute-start | bytes 196616 | tf_op jit(solution)/shard_map/ppermute | solution.py:478
  32.9 3.0 %collective-permute-start.3 = (f32[4,56,128]{2,1,0:T(8,128)S(1)}, f32[4,56,128]{2,1,0:T(8,128)S(1)}, u32[]{:S(2)}, u32[]{:S(2)}) collective-permute-start(f32[4,56,128]{2,1,0:T(8,128)S(1)} %collective-permute-done.1.ra_ref), channel_id=1, source_target_pairs={{0,1},{1,0},{2,3},{3,2},{4,5},{5,4},{6,7},{7,6},{8,9},{9,8},{10,11... | collective-permute-start | bytes 344072 | tf_op jit(solution)/shard_map/ppermute | solution.py:478
  32.9 3.0 %collective-permute-start.4 = (f32[4,56,128]{2,1,0:T(8,128)S(1)}, f32[4,56,128]{2,1,0:T(8,128)S(1)}, u32[]{:S(2)}, u32[]{:S(2)}) collective-permute-start(f32[4,56,128]{2,1,0:T(8,128)S(1)} %collective-permute-done.2.rb_ref), channel_id=1, source_target_pairs={{0,1},{1,0},{2,3},{3,2},{4,5},{5,4},{6,7},{7,6},{8,9},{9,8},{10,11... | collective-permute-start | bytes 344072 | tf_op jit(solution)/shard_map/ppermute | solution.py:478
  33.4 3.3 %collective-permute-start.7 = (f32[4,32,128]{2,1,0:T(8,128)S(1)}, f32[4,32,128]{2,1,0:T(8,128)S(1)}, u32[]{:S(2)}, u32[]{:S(2)}) collective-permute-start(f32[4,32,128]{2,1,0:T(8,128)S(1)} %collective-permute-done.5.sa_ref), channel_id=1, source_target_pairs={{0,1},{1,0},{2,3},{3,2},{4,5},{5,4},{6,7},{7,6},{8,9},{9,8},{10,11... | collective-permute-start | bytes 196616 | tf_op jit(solution)/shard_map/ppermute | solution.py:478
  35.9 1.3 %collective-permute-start.8 = (f32[4,32,128]{2,1,0:T(8,128)S(1)}, f32[4,32,128]{2,1,0:T(8,128)S(1)}, u32[]{:S(2)}, u32[]{:S(2)}) collective-permute-start(f32[4,32,128]{2,1,0:T(8,128)S(1)} %collective-permute-done.6.sb_ref), channel_id=1, source_target_pairs={{0,1},{1,0},{2,3},{3,2},{4,5},{5,4},{6,7},{7,6},{8,9},{9,8},{10,11... | collective-permute-start | bytes 196616 | tf_op jit(solution)/shard_map/ppermute | solution.py:478
  (17 other events, 135.7 us)
where the time goes:
time: 52.6 us; the launch traced here: 52.4 us
  starting transfers between devices  23.3 us (44%)
  Pallas kernels  22.3 us (42%)
  waiting for transfers between devices  3.8 us (7%)
  local copies, waits for them, and re-layouts  2.5 us (5%)
    pallas_call x3, Pallas kernels, call(): pl.pallas_call(kernel, grid=(4,), in_specs=in_specs + [whole(c) for c in...  22.3 us
    ppermute x4, starting transfers between devices, exchange(): return lax.ppermute(value, axis, pairs)  14.5 us
    ppermute x6, starting transfers between devices, partner(): return lax.ppermute(value, 'ens', [(0, 1), (1, 0)])  8.85 us
    ppermute x4, waiting for transfers between devices, exchange(): return lax.ppermute(value, axis, pairs)  2.55 us
    unnamed x78, local copies, waits for them, and re-layouts  2.5 us
    ppermute x6, waiting for transfers between devices, partner(): return lax.ppermute(value, 'ens', [(0, 1), (1, 0)])  1.25 us
  transfers between devices with their start and end apart: 10, of which 3 were waited for; matrix products, arithmetic and copies ran while one was open for 0% of the time, Pallas kernels for 14%

commit v1 on v0

v1 whole, which is shorter than its diff:
```python
import functools
import math

import jax
import jax.numpy as jnp
import ml_dtypes
import numpy as np
from jax import lax
from jax.experimental import pallas as pl
from jax.experimental.pallas import tpu as pltpu
from jax.sharding import PartitionSpec as P

LEVELS = 5
N = 128
EXT = 24

root_three = math.sqrt(3.0)
norm_factor = 4.0 * math.sqrt(2.0)
low_taps = np.array([1.0 + root_three, 3.0 + root_three, 3.0 - root_three, 1.0 - root_three]) / norm_factor
high_taps = np.array([low_taps[3], -low_taps[2], low_taps[1], -low_taps[0]])


def express(rows, basis):
    solved = np.linalg.lstsq(basis.T, rows.T, rcond=1e-9)[0].T
    assert np.abs(solved @ basis - rows).max() < 1e-10
    return solved


def build():
    approx = np.zeros((N + 2, N))
    approx[2:] = np.eye(N)
    A = np.zeros((256, N))
    PM = np.zeros((256, N))
    level = np.zeros(256, int)
    is_low = np.zeros(256, bool)
    valid = np.zeros(256, bool)
    E = np.zeros((EXT, N))
    last = np.zeros((EXT, N))
    last_pm = np.zeros((EXT, N))
    ext_level = np.full(EXT, -1)
    ext_low = np.zeros(EXT, bool)
    S = np.zeros((LEVELS, N))
    T = []
    up = np.zeros((LEVELS, 3, N))
    down = np.zeros((LEVELS, 3, N))
    up_k = np.zeros((LEVELS, 4, 3))
    down_k = np.zeros((LEVELS, 4, 3))
    where_last = np.zeros((LEVELS, 4), int)
    offset, count = 0, N
    for l in range(LEVELS):
        half = count // 2
        bands = []
        for taps in (low_taps, high_taps):
            band = np.zeros((half + 2, N))
            for k in range(-2, half):
                for j in range(4):
                    if -2 <= 2 * k + j < count:
                        band[k + 2] += taps[j] * approx[2 * k + j + 2]
            bands.append(band)
        stride = 2**l
        for b, band in enumerate(bands):
            width = max(half, 8)
            start = offset + width - half
            A[start : start + half] = band[2:]
            valid[start : start + half] = True
            level[offset : offset + width] = l
            is_low[offset : offset + width] = b == 0
            for k in range(half):
                PM[start + k, 2 * stride * k + (0 if b == 0 else stride)] = 1.0
            for k in range(2):
                e = 4 * l + 2 * b + k
                where_last[l, 2 * b + k] = start + half - 2 + k
                ext_level[e], ext_low[e] = l, b == 0
                if l > 0 or k == 1:
                    E[e] = band[k]
                    last[e] = A[start + half - 2 + k]
                    last_pm[e] = PM[start + half - 2 + k]
                else:
                    ext_level[e] = -1
            offset += width
        S[l] = low_taps[2] * approx[2] + low_taps[3] * approx[3]
        t = low_taps[0] * approx[count] + low_taps[1] * approx[count + 1]
        if l == 0:
            T.append(t)
            up[0, 0], down[0, 0] = S[0], t
        else:
            if l == 1:
                T.append(t)
            T += [bands[0][half], bands[1][half]]
            up[l] = np.stack([approx[0], approx[1], S[l]])
            down[l] = np.stack([t, bands[0][half], bands[1][half]])
        up_k[l] = express(E[4 * l : 4 * l + 4], up[l])
        down_k[l] = express(last[4 * l : 4 * l + 4], down[l])
        approx, count = bands[0], half
    T = np.stack(T)
    same = (level[:, None] == level[None, :]) & valid[:, None] & valid[None, :]
    mask = same & ~(is_low[:, None] & is_low[None, :] & (level[:, None] < 4))
    c = {}
    c["A"], c["PM"] = A, PM
    c["E"] = E
    c["S"], c["T"] = S, T
    c["KE"], c["KA"] = express(E, S), express(last, T)
    place = np.zeros((256, EXT))
    for l in range(LEVELS):
        for q in range(4):
            place[where_last[l, q], 4 * l + q] = 1.0
    c["GS"] = (place @ c["KE"]).T
    columns = sorted({int(np.argmax(r)) for r in last_pm if r.any()})
    D = np.zeros((12, N))
    for i, col in enumerate(columns):
        D[i, col] = 1.0
    c["D"] = D
    c["KD"] = last_pm @ D.T
    Y = np.zeros((LEVELS, 8, N))
    PY = np.zeros((LEVELS, 8, N))
    PYC = np.zeros((LEVELS, 8, N))
    for l in range(LEVELS):
        if l == 0:
            Y[0, 3], Y[0, 7] = up[0, 0], down[0, 0]
            PY[0, 4:8] = last_pm[0:4]
        else:
            Y[l, 0:3], Y[l, 4:7] = up[l], down[l]
            PY[l, 0:4] = last_pm[4 * l : 4 * l + 4]
        PYC[l, 0:4] = last_pm[4 * l : 4 * l + 4]
    c["Y"], c["PY"], c["PYC"] = Y.reshape(40, N), PY.reshape(40, N), PYC.reshape(40, N)
    GK = np.zeros((256, 4))
    cup = np.zeros((4, 8, N))
    cdn = np.zeros((4, 8, N))
    hup = np.zeros((4, 8, 96))
    hdn = np.zeros((4, 8, 96))
    lane_level = level[128:]
    ext96 = np.tile(ext_level, 4)
    for l in range(LEVELS):
        for q in range(4):
            for j in range(3):
                row = 3 if l == 0 else j
                if l == 0 and j > 0:
                    continue
                GK[where_last[l, q], row] = up_k[l, q, j]
                if l == 0:
                    cup[3, 4 + q, :] = up_k[0, q, 0]
                    cdn[3, 4 + q, :] = down_k[0, q, 0]
                else:
                    cup[j, q, lane_level == l] = up_k[l, q, j]
                    cdn[j, q, lane_level == l] = down_k[l, q, j]
                hup[row, q, ext96 == l] = up_k[l, q, j]
                hdn[row, q, ext96 == l] = down_k[l, q, j]
    c["GK"] = GK
    c["cup"], c["cdn"], c["hup"], c["hdn"] = cup, cdn, hup, hdn
    c["m0"], c["m1"] = mask[:128, :128], mask[128:, 128:]
    ext_mask = (ext_level[:, None] == level[None, :]) & valid[None, :]
    ext_mask &= ~(ext_low[:, None] & is_low[None, :] & (level[None, :] < 4))
    c["mlh"] = ext_mask
    mth = np.zeros((8, N), bool)
    for q in range(4):
        low = q < 2
        mth[q] = valid[128:] & ~(low & is_low[128:] & (lane_level < 4))
        if q % 2 == 1:
            mth[4 + q] = ~(low & is_low[:128])
    c["mth"] = mth
    mch = np.zeros((8, EXT), bool)
    for q in range(4):
        low = q < 2
        mch[q] = (ext_level >= 0) & ~(low & ext_low & (ext_level < 4))
        mch[q] &= ~((ext_level == 0) & (q % 2 == 0))
    c["mch"] = np.tile(mch, (1, 4))
    c["lane_level"], c["ext_level"] = lane_level, ext_level
    return c


def pad_rows(matrix, rows):
    return np.concatenate([matrix, np.zeros((rows - matrix.shape[0],) + matrix.shape[1:])], 0)


def pad_cols(matrix, cols):
    return pad_rows(matrix.T, cols).T


IMAGES = 16
HX = IMAGES * EXT
X_ROWS = 208
Y_ROWS = 112


@functools.cache
def constants():
    c = build()
    k = {}

    def parts(name, matrix, axis):
        k[name] = ("parts", axis, matrix)

    def exact(name, matrix, axis):
        k[name] = ("exact", axis, matrix)

    def mask(name, array):
        k[name] = ("mask", None, np.asarray(array, np.float64))

    def plain(name, array):
        k[name] = ("plain", None, np.asarray(array, np.float64))

    parts("q_nt", np.concatenate([pad_rows(c["T"], 16), pad_rows(c["S"], 16)]), 1)
    exact("d_nt", pad_rows(c["D"], 16), 1)
    parts("at", c["A"].T, 0)
    parts("gs", pad_rows(c["GS"], 16), 0)
    fours = np.kron(np.eye(4), np.concatenate([c["KE"], np.zeros((EXT, 5))], 1))
    parts("kz", pad_cols(np.concatenate([np.kron(np.eye(4), c["KA"]), fours], 1), 128), 1)
    exact("kd", pad_cols(np.kron(np.eye(4), c["KD"]), 128), 1)
    parts("y_nt", pad_rows(c["Y"], 48), 1)
    exact("pt", c["PM"].T, 0)
    exact("p0", c["PM"][:128], 1)
    exact("p1", c["PM"][128:], 1)
    exact("py", pad_rows(c["PY"], 48), 1)
    exact("pyc_nt", pad_rows(c["PYC"], 48), 1)
    gst = np.zeros((128, 256))
    for i in range(8):
        gst[10 * i : 10 * i + 5] = c["GS"]
    parts("gst", gst, 0)
    kdb = np.zeros((128, 128))
    for i in range(4):
        kdb[12 * i : 12 * i + 12, EXT * i : EXT * (i + 1)] = c["KD"].T
    exact("kdb", kdb, 0)
    own = np.zeros((8, 8, 128))
    for i in range(8):
        own[i, :, 10 * i : 10 * i + 10] = 1.0
    mask("own", own)
    parts("gkt", pad_cols(c["GK"], 16).T, 0)
    left = np.arange(N) < 64
    w = np.zeros((9, 4, 8, N))
    for j in range(4):
        g = c["GK"][:, j : j + 1]
        w[0, j] = np.where(left, g[152:160], 0)
        w[1, j] = np.where(left, g[184:192], g[56:64])
        w[2, j] = g[120:128]
        for n, start in enumerate((200, 216, 224, 232, 240, 248)):
            w[3 + n, j] = g[start : start + 8]
    assert np.isclose(np.abs(w[..., 0]).sum() + np.abs(c["GK"][56:64]).sum(), np.abs(c["GK"]).sum())
    plain("gkc", w)
    top = np.concatenate([np.where(left[:, None], 0, c["A"][:N]), np.where(left[:, None], c["A"][N:], 0)], 1)
    parts("st", top, 0)
    parts("s0", c["A"][:128], 0)
    parts("s1", c["A"][128:], 0)
    upper = np.where(left, c["m1"][:64], c["m0"][:64])
    mask("mf", np.concatenate([upper, c["m0"][64:]]))
    mask("ml", c["m1"][64:])
    parts("e_tn", pad_rows(c["E"], 32), 0)
    ey = np.zeros((128, N))
    ey[4:8] = c["E"][0:4]
    for l in range(1, LEVELS):
        ey[8 * l : 8 * l + 4] = c["E"][4 * l : 4 * l + 4]
    parts("o", np.concatenate([c["A"].T, ey.T], 1), 1)
    plain("cup", c["cup"])
    plain("cdn", c["cdn"])
    plain("hup", np.tile(c["hup"][:, :, :EXT], (1, 1, IMAGES)))
    plain("hdn", np.tile(c["hdn"][:, :, :EXT], (1, 1, IMAGES)))
    lane = c["lane_level"]
    ext = np.tile(c["ext_level"], IMAGES)
    mask("fold", np.stack([np.broadcast_to(lane == l, (8, N)) for l in range(1, LEVELS)]))
    mask("foldx", np.stack([np.broadcast_to(ext == l, (8, HX)) for l in range(LEVELS)]))
    mask("mlh", c["mlh"])
    mask("mth", c["mth"])
    mask("mch", np.tile(c["mch"][:, :EXT], (1, 8)))
    tl = np.zeros((LEVELS, 8, N))
    tl[0, 4:8] = 1.0
    for l in range(1, LEVELS):
        tl[l, 0:4, lane == l] = 1.0
    mask("tl", tl)
    cl = np.zeros((LEVELS, 8, 3, 32))
    for l in range(LEVELS):
        cl[l, slice(4, 8) if l == 0 else slice(0, 4), :, :EXT] = c["ext_level"] == l
    mask("cl", cl.reshape(LEVELS, 8, 96))
    return k


def pieces(array, tile):
    array = array.reshape((-1,) + array.shape[-2:])
    width = -(-array.shape[2] // N) * N
    height = -(-array.shape[1] // tile) * tile
    full = np.zeros((array.shape[0], height, width))
    full[:, : array.shape[1], : array.shape[2]] = array
    return full.reshape(array.shape[0], height, width // N, N).transpose(0, 2, 1, 3)


@functools.cache
def packed(names):
    narrow, wide, places = [np.zeros((16, N))], [np.zeros((16, N))], {}
    for name in names:
        kind, axis, array = constants()[name]
        into = wide if kind == "plain" else narrow
        blocks = pieces(array, 8 if kind == "plain" else 16)
        places[name] = (kind, axis, sum(g.shape[0] for g in into), blocks.shape, array.shape)
        if kind == "parts":
            high = blocks.astype(ml_dtypes.bfloat16).astype(np.float64)
            into += [high.reshape(-1, N), (blocks - high).reshape(-1, N)]
        else:
            into.append(blocks.reshape(-1, N))
    arrays = [np.concatenate(narrow).astype(ml_dtypes.bfloat16), np.concatenate(wide).astype(np.float32)]
    return arrays, places


def reader(names, refs):
    places = packed(names)[1]

    def read(name, *index):
        kind, axis, start, blocks, shape = places[name]
        ref = refs[1] if kind == "plain" else refs[0]
        count, columns, height, _ = blocks
        at = 0
        for dim, value in zip(shape, index):
            at = at * dim + value
        assert np.prod(shape[: len(index)], dtype=int) == count

        def one(base):
            first = [base + (at * columns + j) * height for j in range(columns)]
            block = jnp.concatenate([ref[f : f + height, :] for f in first], 1)
            return block

        if kind == "parts":
            high, low = one(start), one(start + count * columns * height)
            return jnp.concatenate([high, high, low], axis)
        if kind == "exact":
            return jnp.concatenate([one(start)] * 2, axis)
        return one(start).astype(jnp.float32)[: shape[-2], : shape[-1]]

    return read


def split(x):
    high = x.astype(jnp.bfloat16).astype(jnp.float32)
    return high, x - high


def data3(x, axis):
    high, low = split(x)
    return jnp.concatenate([high, low, high], axis).astype(jnp.bfloat16)


def data2(x, axis):
    high, low = split(x)
    return jnp.concatenate([high, low], axis).astype(jnp.bfloat16)


def nn(a, b):
    return lax.dot_general(a, b, (((1,), (0,)), ((), ())), preferred_element_type=jnp.float32)


def nt(a, b):
    return lax.dot_general(a, b, (((1,), (1,)), ((), ())), preferred_element_type=jnp.float32)


def tn(a, b):
    return lax.dot_general(a, b, (((0,), (0,)), ((), ())), preferred_element_type=jnp.float32)


def lanes(x, i):
    return x[:, N * i : N * (i + 1)]


def rows(x, i):
    return x[N * i : N * (i + 1)]


def side_by_side(x):
    return jnp.concatenate([rows(x, i) for i in range(x.shape[0] // N)], 1)


def zeros(*shape):
    return jnp.zeros(shape, jnp.float32)


def wider(x, width):
    return jnp.concatenate([x, zeros(x.shape[0], width - x.shape[1])], 1)


def taller(x, height):
    return jnp.concatenate([x, zeros(height - x.shape[0], x.shape[1])], 0)


def even_place(axis):
    return lax.axis_index(axis) % 2 == 0


HALF = 64
H = [float(t) for t in low_taps]
G = [float(t) for t in high_taps]


FIRST = ("q_nt", "d_nt")


def first_kernel(x_hbm, clim_hbm, q_hbm, a_ref, b_ref, s_ref, x_ref, clim_ref, q_ref, sems):
    even = even_place("tx")
    ens = lax.axis_index("ens")
    pairs = [(q_hbm, q_ref)]
    for m in range(2):
        for h in range(2):
            pairs.append((x_hbm.at[m, pl.ds(4 * h, 4)], x_ref.at[m, pl.ds(4 * h, 4)]))
    pairs.append((clim_hbm, clim_ref))
    copies = [pltpu.make_async_copy(src, dst, sems.at[i]) for i, (src, dst) in enumerate(pairs)]
    for copy in copies:
        copy.start()
    copies[0].wait()
    k = reader(FIRST, (q_ref,))
    q = k("q_nt")
    right, left = [], []
    for g in range(4):
        copies[1 + g].wait()
        x3 = data3(x_ref[g // 2, 4 * (g % 2) : 4 * (g % 2) + 4].reshape(4 * N, N), 1)
        u = nt(q, x3)
        right += [lanes(u, i)[0:10] for i in range(4)]
        left += [lanes(u, i)[16:26] for i in range(4)]
    copies[5].wait()
    d = nt(k("d_nt"), data2(clim_ref[pl.ds(4 * ens, 4)].reshape(4 * N, N), 1))
    right += [lanes(d, j)[0:12] for j in range(4)]
    left = jnp.concatenate(left, 0)
    s_ref[...] = left
    right, left = jnp.concatenate(right, 0), taller(left, X_ROWS)
    a_ref[...] = jnp.where(even, right, left)
    b_ref[...] = jnp.where(even, left, right)


BESIDE = (
    "at", "fold", "foldx", "gst", "kdb", "kz", "mf", "ml", "own", "p0", "p1", "pt", "py", "pyc_nt",
    "y_nt",
)


def beside_kernel(x_ref, clim_ref, *refs):
    n = 2
    k = reader(BESIDE, refs[:n])
    z_ref, s_ref, c_ref, cf_ref, cl_ref = refs[n:]
    ens = lax.axis_index("ens")
    at = k("at")
    for g in range(4):
        x = x_ref[g // 2, 4 * (g % 2) : 4 * (g % 2) + 4].reshape(4 * N, N)
        z_ref[4 * N * g : 4 * N * (g + 1), :] = nn(data3(x, 1), at)
        y = nn(k("y_nt"), data3(side_by_side(x), 0))
        y = jnp.concatenate([lanes(y, i)[0:40] for i in range(4)], 0)
        y = nn(data3(y, 1), at)
        for i in range(4):
            strip = y[40 * i : 40 * i + 8, :N]
            for l in range(4):
                strip = strip + k("fold", l) * y[40 * i + 8 * l + 8 : 40 * i + 8 * l + 16, N:]
            s_ref[8 * (4 * g + i) : 8 * (4 * g + i) + 8, :] = strip
    clim = clim_ref[pl.ds(4 * ens, 4)].reshape(4 * N, N)
    y = nn(k("py"), data2(side_by_side(clim), 0))
    y = jnp.concatenate([lanes(y, i)[0:40] for i in range(4)], 0)
    y = nn(data2(y, 1), k("pt"))
    for i in range(4):
        strip = y[40 * i : 40 * i + 8, :N]
        for l in range(4):
            strip = strip + k("fold", l) * y[40 * i + 8 * l + 8 : 40 * i + 8 * l + 16, N:]
        c_ref[8 * i : 8 * i + 8, :] = strip
    inside = lax.broadcasted_iota(jnp.int32, (HALF, N), 1) < HALF
    for g in range(2):
        cz = nn(data2(clim_ref[4 * g : 4 * g + 4].reshape(4 * N, N), 1), k("pt"))
        c0 = nn(k("p0"), data2(side_by_side(cz[:, :N]), 0))
        c1 = nn(k("p1"), data2(side_by_side(cz[:, N:]), 0))
        for j in range(4):
            w0, w1 = lanes(c0, j), lanes(c1, j)
            upper = jnp.where(inside, w1[:HALF], w0[:HALF])
            cf_ref[4 * g + j] = 0.5 * k("mf") * jnp.concatenate([upper, w0[HALF:]], 0)
            cl_ref[4 * g + j] = 0.5 * k("ml") * w1[HALF:]


SECOND = (
    "fold", "foldx", "gst", "kdb", "kz", "own", "pyc_nt", "y_nt",
)


def second_kernel(ra_ref, rb_ref, sx_ref, s_ref, c_ref, *refs):
    n = 2
    k = reader(SECOND, refs[:n])
    a_ref, b_ref, up_ref, right_ref, left_ref = refs[n:]
    kz = k("kz")
    even, even_y = even_place("tx"), even_place("ty")
    ra, rb = ra_ref[...], rb_ref[...]
    from_right, from_left = jnp.where(even, ra[:160], rb[:160]), jnp.where(even, rb, ra)
    right_ref[...] = from_right
    strips = []
    for g in range(2):
        f = taller(from_right[80 * g : 80 * g + 80], 128)
        y = nt(k("y_nt"), data3(f, 1))[0:40]
        spread = jnp.concatenate(
            [k("own", i) * y[8 * l : 8 * l + 8] for i in range(8) for l in range(LEVELS)], 0
        )
        t = nn(data3(spread, 1), k("gst"))
        for i in range(8):
            at = 40 * i
            strip = s_ref[64 * g + 8 * i : 64 * g + 8 * i + 8, :] + t[at : at + 8, :N]
            for l in range(4):
                strip = strip + k("fold", l) * t[at + 8 * l + 8 : at + 8 * l + 16, N:]
            strips.append(strip)
    for g in range(4):
        f = jnp.concatenate([from_left[40 * g : 40 * g + 40], sx_ref[40 * g : 40 * g + 40]], 0)
        left_ref[96 * g : 96 * g + 96] = nn(kz, data3(taller(f, 128), 0))
    left_ref[384:432] = from_left[160:208]
    hy = nt(k("y_nt"), data3(left_ref[0:384], 1))
    corner = sum(k("foldx", l) * hy[8 * l : 8 * l + 8] for l in range(LEVELS))
    cx = nt(k("pyc_nt"), data2(taller(from_left[160:208], 128), 1))[0:40]
    cc = nn(data2(cx, 1), k("kdb"))
    cc = sum(k("foldx", l)[:, :N] * cc[8 * l : 8 * l + 8] for l in range(LEVELS))
    up = [s[0:4] for s in strips] + [lanes(corner, g)[0:4] for g in range(3)] + [zeros(36, N)]
    down = [s[4:8] for s in strips] + [lanes(corner, g)[4:8] for g in range(3)] + [cc[0:4], c_ref[...]]
    up, down = jnp.concatenate(up, 0), jnp.concatenate(down, 0)
    a_ref[...] = jnp.where(even_y, down, up)
    b_ref[...] = jnp.where(even_y, up, down)
    up_ref[...] = up


def filtered(ref, count):
    parts = [ref[pl.ds(j, count, stride=2), :] for j in range(4)]
    low = H[0] * parts[0] + H[1] * parts[1] + H[2] * parts[2] + H[3] * parts[3]
    high = G[0] * parts[0] + G[1] * parts[1] + G[2] * parts[2] + G[3] * parts[3]
    return low, high


THIRD = (
    "at", "gs", "kd", "mlh", "pt",
)


def third_kernel(z_ref, xp_ref, fr_ref, fl_ref, frp_ref, flp_ref, *refs):
    n = 2
    k = reader(THIRD, refs[:n])
    wf_ref, wl_ref, lh_ref, clh_ref, order_ref = refs[n : n + 5]
    z0_buf, z1_buf, a_buf, b_buf, c_buf, d_buf = refs[n + 5 :]
    first = lax.axis_index("ens") == 0
    inside = lax.broadcasted_iota(jnp.int32, (HALF, N), 1) < HALF
    at = k("at")
    for side, (fr, fl) in enumerate(((fr_ref, fl_ref), (frp_ref, flp_ref))):
        for g in range(4):
            where = 40 * g
            f = jnp.concatenate([fr[where + 10 * i : where + 10 * i + 5] for i in range(4)], 1)
            z = tn(data3(taller(f, 16), 0), k("gs"))
            if side == 0:
                z = z + z_ref[4 * N * g : 4 * N * (g + 1), :]
            else:
                x = xp_ref[g // 2, 4 * (g % 2) : 4 * (g % 2) + 4].reshape(4 * N, N)
                z = z + nn(data3(x, 1), at)
            zl = fl[96 * g : 96 * g + 96]
            lh_ref[side, 4 * g : 4 * g + 4] = nn(data3(zl, 1), at).reshape(4, EXT, 256)
            for i in range(4):
                image = 4 * g + i
                slot = 16 * side + image
                z0_buf[slot, 0:N] = rows(z, i)[:, :N]
                z1_buf[slot, 0:N] = rows(z, i)[:, N:]
                z0_buf[slot, N : N + 8] = zeros(8, N)
                z1_buf[slot, N : N + 8] = zeros(8, N)
                low0, high0 = filtered(z0_buf.at[slot], 64)
                a_buf[slot, 0:64] = filtered(z1_buf.at[slot], 64)[0]
                a_buf[slot, 64:72] = zeros(8, N)
                low1, high1 = filtered(a_buf.at[slot], 32)
                b_buf[slot, 0:32] = low1
                b_buf[slot, 32:40] = zeros(8, N)
                low2, high2 = filtered(b_buf.at[slot], 16)
                c_buf[slot, 0:16] = low2
                c_buf[slot, 16:24] = zeros(8, N)
                low3, high3 = filtered(c_buf.at[slot], 8)
                d_buf[slot, 0:8] = low3
                d_buf[slot, 8:16] = zeros(8, N)
                low4, high4 = filtered(d_buf.at[slot], 4)
                wf_ref[side, image, 0:64] = jnp.where(inside, jnp.concatenate([low1, high1], 0), low0)
                wf_ref[side, image, 64:128] = high0
                wl_ref[side, image] = jnp.concatenate(
                    [low2, high2, low3, high3, zeros(4, N), low4, zeros(4, N), high4], 0
                )
    mine, other = fl_ref[384:432], flp_ref[384:432]
    halos = [jnp.where(first, mine, other), jnp.where(first, other, mine)]
    for g in range(2):
        cl = nn(k("kd"), data2(taller(halos[g], 128), 0))
        clh = nn(data2(cl, 1), k("pt"))
        for j in range(4):
            clh_ref[4 * g + j] = 0.5 * k("mlh") * clh[EXT * j : EXT * (j + 1)]
    order_ref[...] = zeros(8, N)


def sort_kernel(sa_ref, sb_ref, order_ref, out_ref):
    even_y = even_place("ty")
    a, b = sa_ref[...], sb_ref[...]
    out_ref[0:80] = jnp.where(even_y, a, b)[0:80]
    out_ref[80:192] = jnp.where(even_y, b, a)


FOURTH = (
    "cdn", "cl", "cup", "e_tn", "gkc", "gkt", "hdn", "hup", "mch", "mf", "ml", "mlh", "mth", "o",
    "s0", "s1", "st", "tl",
)


def fourth_kernel(wf_ref, wl_ref, lh_ref, cf_ref, cl_ref, clh_ref, got_ref, gotp_ref, up_ref, upp_ref, *refs):
    n = 2
    k = reader(FOURTH, refs[:n])
    out_ref = refs[n]
    first = lax.axis_index("ens") == 0
    belows, aboves, ups, lhs, chs = [], [], [], [], []
    for got, up in ((got_ref, up_ref), (gotp_ref, upp_ref)):
        below, above, up = got[0:80], got[80:192], up[...]
        hb = jnp.concatenate([below[64 + 4 * g : 68 + 4 * g] for g in range(3)], 1)
        lhs.append(tn(data3(taller(hb, 16), 0), k("gkt")))
        hu = jnp.concatenate([up[64 + 4 * g : 68 + 4 * g] for g in range(3)], 1)
        hd = jnp.concatenate([above[64 + 4 * g : 68 + 4 * g] for g in range(3)], 1)
        ch = zeros(8, HX)
        for j in range(4):
            ch = ch + k("hup", j) * hu[j : j + 1] + k("hdn", j) * hd[j : j + 1]
        belows.append(below)
        aboves.append(above)
        ups.append(up)
        chs.append(ch)
    halos = [jnp.where(first, aboves[0], aboves[1])[76:112], jnp.where(first, aboves[1], aboves[0])[76:112]]

    def top(side, i):
        t = zeros(8, N)
        for j in range(4):
            at = 4 * i + j
            t = t + k("cup", j) * ups[side][at : at + 1] + k("cdn", j) * aboves[side][at : at + 1]
        return t

    def grown(w, side, i, groups):
        parts, done = [], 0
        for start, which, js in groups:
            if start > done:
                parts.append(w[done:start])
            part = w[start : start + 8]
            for j in js:
                part = part + k("gkc", which, j) * belows[side][4 * i + j : 4 * i + j + 1]
            parts.append(part)
            done = start + 8
        return jnp.concatenate(parts + ([w[done:]] if done < w.shape[0] else []), 0)

    def variance(half_clim, mask, parts):
        total = parts[0] * parts[0]
        for part in parts[1:]:
            total = total + part * part
        return half_clim + (0.125 * mask) * total

    in_full = ((24, 0, (0, 1, 2)), (56, 1, (0, 1, 2, 3)), (120, 2, (3,)))
    in_rest = tuple((start, 3 + n, (0, 1, 2)) for n, start in enumerate((8, 24, 32, 40, 48, 56)))
    cch = jnp.concatenate([h[0:4, 0:96] for h in halos], 1)
    cch = jnp.concatenate([cch, zeros(4, 192)], 0)
    vch = variance(0.5 * k("mch") * cch, k("mch"), [c[:, 192 * m : 192 * m + 192] for c in chs for m in range(2)])
    sch = [chs[0][:, 192 * m : 192 * m + 192] * vch for m in range(2)]
    sch = [wider(s, 256) for s in sch]
    edge = []
    for i in range(IMAGES):
        at = EXT * (i % 8)
        c = sch[i // 8][0:4, at : at + EXT]
        edge.append(jnp.concatenate([c, c], 0))
    high, low = split(wider(jnp.concatenate(edge, 0), 32))
    edge = jnp.concatenate([high, low, high], 1)
    edge = jnp.concatenate([k("cl", l) * edge[8 * i : 8 * i + 8] for l in range(LEVELS) for i in range(IMAGES)], 0)
    tu_edge = nn(edge.astype(jnp.bfloat16), k("e_tn"))
    for g in range(4):
        sf, sl, slh, sth = [None] * 4, [None] * 4, [None] * 4, [None] * 4
        for n in range(2):
            v = 2 * g + n
            four = [(side, v + 8 * m) for side in range(2) for m in range(2)]
            wf = [grown(wf_ref[side, i], side, i, in_full) for side, i in four]
            wl = [grown(wl_ref[side, i], side, i, in_rest) for side, i in four]
            lh = [lh_ref[side, i] + lhs[side][EXT * i : EXT * (i + 1)] for side, i in four]
            th = [top(side, i) for side, i in four]
            vf = variance(cf_ref[v], k("mf"), wf)
            vl = variance(cl_ref[v], k("ml"), wl)
            vlh = variance(clh_ref[v], k("mlh"), lh)
            climth = halos[v // 4][4 + 8 * (v % 4) : 12 + 8 * (v % 4)]
            vth = variance(0.5 * k("mth") * climth, k("mth"), th)
            for m in range(2):
                sf[2 * m + n] = wf[m] * vf
                sl[2 * m + n] = wl[m] * vl
                slh[2 * m + n] = lh[m] * vlh
                sth[2 * m + n] = th[m] * vth
        upper = nn(data3(jnp.concatenate([s[:HALF] for s in sf], 0), 1), k("st"))
        lower = nn(data3(jnp.concatenate([s[HALF:] for s in sf], 0), 1), k("s0"))
        rest = nn(data3(jnp.concatenate(sl, 0), 1), k("s1"))
        top0 = jnp.concatenate([k("tl", 0) * sth[i] for i in range(4)], 0)
        top1 = jnp.concatenate([k("tl", l) * sth[i] for l in range(1, LEVELS) for i in range(4)], 0)
        tu = jnp.concatenate([nn(data3(top0, 1), k("s0")), nn(data3(top1, 1), k("s1"))], 0)
        full = []
        for i in range(4):
            r = tn(data3(taller(slh[i], 32), 0), k("e_tn"))
            at = HALF * i
            parts = [upper[at : at + HALF, :N], lower[at : at + HALF], upper[at : at + HALF, N:], rest[at : at + HALF]]
            t = []
            for l in range(LEVELS):
                edge = 128 * l + 8 * (8 * (i // 2) + 2 * g + i % 2)
                t.append(tu[8 * (4 * l + i) : 8 * (4 * l + i) + 8] + tu_edge[edge : edge + 8])
            t.append(zeros(88, N))
            full.append(jnp.concatenate([jnp.concatenate(parts, 0) + r] + t, 0))
        out = nn(k("o"), data3(jnp.concatenate(full, 1), 0))
        for i in range(4):
            out_ref[i // 2, 2 * g + i % 2] = lanes(out, i)


VMEM = pl.BlockSpec(memory_space=pltpu.VMEM)


def call(kernel, arguments, shapes, flops, scratch=(), in_specs=None, limit=40):
    return pl.pallas_call(
        kernel,
        in_specs=in_specs or [VMEM] * len(arguments),
        out_specs=[VMEM] * len(shapes),
        out_shape=[s if hasattr(s, "dtype") else jax.ShapeDtypeStruct(s, jnp.float32) for s in shapes],
        scratch_shapes=scratch,
        cost_estimate=pl.CostEstimate(flops=flops, bytes_accessed=1 << 20, transcendentals=0),
        compiler_params=pltpu.CompilerParams(vmem_limit_bytes=limit * 1024 * 1024),
    )(*arguments)


def exchange(value, axis, odd):
    count = lax.axis_size(axis)
    pairs = [(i, (i + 1 if i % 2 == odd else i - 1) % count) for i in range(count)]
    return lax.ppermute(value, axis, pairs)


def partner(value):
    return lax.ppermute(value, "ens", [(0, 1), (1, 0)])


def buffer(count, height):
    return pltpu.VMEM((count, height, N), jnp.float32)


def held(names):
    return [jnp.asarray(array) for array in packed(names)[0]]


def shards(x_hbm, clim_hbm):
    xp = partner(x_hbm)
    m1, m2 = (X_ROWS, N), (Y_ROWS, N)
    q = held(FIRST)[0]
    hbm = pl.BlockSpec(memory_space=pltpu.HBM)
    xa, xb, sx, x, clim = call(
        first_kernel,
        (x_hbm, clim_hbm, q),
        [m1, m1, (160, N), x_hbm.shape, clim_hbm.shape],
        10**8,
        [pltpu.VMEM(q.shape, q.dtype), pltpu.SemaphoreType.DMA((6,))],
        [hbm] * 3,
        60,
    )
    ra, rb = exchange(xa, "tx", 0), exchange(xb, "tx", 1)
    z, strips, tops, cf, cl = call(
        beside_kernel,
        (x, clim, *held(BESIDE)),
        [(IMAGES * N, 256), (IMAGES * 8, N), (32, N), (8, N, N), (8, HALF, N)],
        10**9,
    )
    ya, yb, up, fr, fl = call(
        second_kernel, (ra, rb, sx, strips, tops, *held(SECOND)), [m2, m2, m2, (160, N), (432, N)], 10**9
    )
    sa, sb = exchange(ya, "ty", 0), exchange(yb, "ty", 1)
    frp, flp, upp = partner(fr), partner(fl), partner(up)
    wf, wl, lh, clh, order = call(
        third_kernel,
        (z, xp, fr, fl, frp, flp, *held(THIRD)),
        [(2, IMAGES, N, N), (2, IMAGES, HALF, N), (2, IMAGES, EXT, 256), (8, EXT, 256), (8, N)],
        2 * 10**9,
        [buffer(32, h) for h in (136, 136, 72, 40, 24, 16)],
    )
    got = call(sort_kernel, (sa, sb, order), [(192, N)], 10**6)[0]
    gotp = partner(got)
    arguments = (wf, wl, lh, cf, cl, clh, got, gotp, up, upp, *held(FOURTH))
    return call(fourth_kernel, arguments, [x_hbm.shape], 10**9)[0]


def solution(mesh):
    in_specs = (P("ens", None, "ty", "tx"), P(None, "ty", "tx"))
    out_specs = P("ens", None, "ty", "tx")
    return jax.shard_map(shards, mesh=mesh, in_specs=in_specs, out_specs=out_specs, check_vma=False)
```

time: 52.6 us -> 37 us (0.70)
  Pallas kernels: 22.3 us -> 13.3 us
  starting transfers between devices: 23.3 us -> 18.9 us
  waiting for transfers between devices: 3.8 us -> 0.98 us
  local copies, waits for them, and re-layouts: 2.5 us -> 3.39 us
    pallas_call x3 -> x6, Pallas kernels: 22.3 us -> 13.3 us  [call(): pl.pallas_call(kernel, in_specs=in_specs or [VMEM] * len(arguments), out_...]
    ppermute x6 -> x5, starting transfers between devices: 8.85 us -> 6.12 us  [partner(): return lax.ppermute(value, 'ens', [(0, 1), (1, 0)])]
    ppermute x4, waiting for transfers between devices: 2.55 us -> 0.01 us  [exchange(): return lax.ppermute(value, axis, pairs)]
    ppermute x4, starting transfers between devices: 14.5 us -> 12.8 us  [exchange(): return lax.ppermute(value, axis, pairs)]
    unnamed x78 -> x16, local copies, waits for them, and re-layouts: 2.5 us -> 3.39 us
    ppermute x6 -> x5, waiting for transfers between devices: 1.25 us -> 0.97 us  [partner(): return lax.ppermute(value, 'ens', [(0, 1), (1, 0)])]
  transfers between devices with their start and end apart: 10 -> 9, of which waited for: 3 -> 1; matrix products, arithmetic and copies ran while one was open for 0% -> 0% of each run, Pallas kernels for 14% -> 25%
where the time goes in v1:
time: 37 us; the launch traced here: 36.8 us
  starting transfers between devices  18.9 us (51%)
  Pallas kernels  13.3 us (36%)
  local copies, waits for them, and re-layouts  3.39 us (9%)
  waiting for transfers between devices  0.98 us (3%)
    pallas_call x6, Pallas kernels, call(): pl.pallas_call(kernel, in_specs=in_specs or [VMEM] * len(arguments), out_...  13.3 us
    ppermute x4, starting transfers between devices, exchange(): return lax.ppermute(value, axis, pairs)  12.8 us
    ppermute x5, starting transfers between devices, partner(): return lax.ppermute(value, 'ens', [(0, 1), (1, 0)])  6.12 us
    unnamed x16, local copies, waits for them, and re-layouts  3.39 us
    ppermute x5, waiting for transfers between devices, partner(): return lax.ppermute(value, 'ens', [(0, 1), (1, 0)])  0.97 us
  transfers between devices with their start and end apart: 9, of which 1 were waited for; matrix products, arithmetic and copies ran while one was open for 0% of the time, Pallas kernels for 25%

profile of v1, /device:TPU:1, one launch (start us, length us, event | category | flops | bytes accessed | tf_op | source)
XLA Modules:
  0.0 36.8 jit_solution(5941041279646738025)
XLA Ops:
  0.0 3.2 %collective-permute-start = (f32[2,8,128,128]{3,2,1,0:T(8,128)}, f32[2,8,128,128]{3,2,1,0:T(8,128)S(1)}, u32[]{:S(2)}, u32[]{:S(2)}) collective-permute-start(f32[2,8,128,128]{3,2,1,0:T(8,128)} %x_hbm.1), channel_id=1, source_target_pairs={{0,1},{1,0},{2,3},{3,2},{4,5},{5,4},{6,7},{7,6},{8,9},{9,8},{10,11... | collective-permute-start | bytes 3145736 | tf_op jit(solution)/shard_map/ppermute | solution.py:716
  3.2 3.2 %shard_map.109 = (f32[208,128]{1,0:T(8,128)}, f32[208,128]{1,0:T(8,128)}, f32[160,128]{1,0:T(8,128)}, f32[2,8,128,128]{3,2,1,0:T(8,128)}, f32[8,128,128]{2,1,0:T(8,128)}) custom-call(f32[2,8,128,128]{3,2,1,0:T(8,128)} %x_hbm.1, f32[8,128,128]{2,1,0:T(8,128)} %clim_hbm.1, bf16[96,128]{1,0:T(8,128)(2,1)} %constant.14.clone.q_hbm), custom_call_target="tpu_custom_call" | custom-call | flops 100000000 | bytes 1048576 | tf_op jit(solution)/shard_map/pallas_call | solution.py:698
  6.5 0.1 collective-permute-start.1
  6.6 5.5 %collective-permute-start.2 = (f32[208,128]{1,0:T(8,128)}, f32[208,128]{1,0:T(8,128)S(1)}, u32[]{:S(2)}, u32[]{:S(2)}) collective-permute-start(f32[208,128]{1,0:T(8,128)} %get-tuple-element.29), channel_id=1, source_target_pairs={{0,30},{2,4},{4,2},{6,8},{8,6},{10,12},{12,10},{14,16},{16,14},{18... | collective-permute-start | bytes 319496 | tf_op jit(solution)/shard_map/ppermute | solution.py:712
  12.1 1.2 %copy-done.2 = f32[2,8,128,128]{3,2,1,0:T(8,128)S(1)} copy-done((f32[2,8,128,128]{3,2,1,0:T(8,128)S(1)}, f32[2,8,128,128]{3,2,1,0:T(8,128)}, u32[]{:S(2)}) %copy-start.2) | copy-done | bytes 1048600
  13.3 1.0 %copy-done.3 = f32[8,128,128]{2,1,0:T(8,128)S(1)} copy-done((f32[8,128,128]{2,1,0:T(8,128)S(1)}, f32[8,128,128]{2,1,0:T(8,128)}, u32[]{:S(2)}) %copy-start.3) | copy-done | bytes 524312
  14.4 1.1 %copy-done.5 = bf16[2688,128]{1,0:T(8,128)(2,1)S(1)} copy-done((bf16[2688,128]{1,0:T(8,128)(2,1)S(1)}, bf16[2688,128]{1,0:T(8,128)(2,1)}, u32[]{:S(2)}) %copy-start.5) | copy-done | bytes 688152
  15.5 2.0 %shard_map.110 = (f32[2048,256]{1,0:T(8,128)S(1)}, f32[128,128]{1,0:T(8,128)S(1)}, f32[32,128]{1,0:T(8,128)S(1)}, f32[8,128,128]{2,1,0:T(8,128)S(1)}, f32[8,64,128]{2,1,0:T(8,128)S(1)}) custom-call(f32[2,8,128,128]{3,2,1,0:T(8,128)S(1)} %copy-done.2, f32[8,128,128]{2,1,0:T(8,128)S(1)} %copy-done.3, bf16[2688,128]{1,0:T(8,128)(2,1)S(1)} %copy-done.5, ...), custom_call_target="tpu_custom_call" | custom-call | flops 1000000000 | bytes 1048576 | tf_op jit(solution)/shard_map/pallas_call | solution.py:698
  17.5 0.0 copy-start.7
  17.5 0.0 collective-permute-done.1.ra_ref
  17.5 0.0 collective-permute-done.2.rb_ref
  17.5 0.0 copy-done.6
  17.5 0.0 copy-done.4
  17.5 0.9 %shard_map.111 = (f32[112,128]{1,0:T(8,128)S(1)}, f32[112,128]{1,0:T(8,128)S(1)}, f32[112,128]{1,0:T(8,128)S(1)}, f32[160,128]{1,0:T(8,128)S(1)}, f32[432,128]{1,0:T(8,128)S(1)}) custom-call(f32[208,128]{1,0:T(8,128)S(1)} %collective-permute-done.1.ra_ref, f32[208,128]{1,0:T(8,128)S(1)} %collective-permute-done.2.rb_ref, f32[160,128]{1,0:T(8,128)S(1)} %copy-done.4, ...), custom_call_target="tpu_custom_call" | custom-call | flops 1000000000 | bytes 1048576 | tf_op jit(solution)/shard_map/pallas_call | solution.py:698
  18.5 0.6 %collective-permute-start.4 = (f32[432,128]{1,0:T(8,128)S(1)}, f32[432,128]{1,0:T(8,128)S(1)}, u32[]{:S(2)}, u32[]{:S(2)}) collective-permute-start(f32[432,128]{1,0:T(8,128)S(1)} %get-tuple-element.34.fl_ref), channel_id=1, source_target_pairs={{0,1},{1,0},{2,3},{3,2},{4,5},{5,4},{6,7},{7,6},{8,9},{9,8},{10,11... | collective-permute-start | bytes 663560 | tf_op jit(solution)/shard_map/ppermute | solution.py:716
  19.1 0.1 collective-permute-start.3
  19.2 1.2 %collective-permute-start.5 = (f32[112,128]{1,0:T(8,128)S(1)}, f32[112,128]{1,0:T(8,128)S(1)}, u32[]{:S(2)}, u32[]{:S(2)}) collective-permute-start(f32[112,128]{1,0:T(8,128)S(1)} %get-tuple-element.41), channel_id=1, source_target_pairs={{0,32},{32,0},{64,96},{96,64},{128,160},{160,128},{192,224},{224,1... | collective-permute-start | bytes 172040 | tf_op jit(solution)/shard_map/ppermute | solution.py:712
  20.4 6.0 %collective-permute-start.6 = (f32[112,128]{1,0:T(8,128)S(1)}, f32[112,128]{1,0:T(8,128)S(1)}, u32[]{:S(2)}, u32[]{:S(2)}) collective-permute-start(f32[112,128]{1,0:T(8,128)S(1)} %get-tuple-element.42), channel_id=1, source_target_pairs={{0,224},{32,64},{64,32},{96,128},{128,96},{160,192},{192,160},{224... | collective-permute-start | bytes 172040 | tf_op jit(solution)/shard_map/ppermute | solution.py:712
  26.4 0.0 collective-permute-done.3.frp_ref
  26.4 0.0 collective-permute-done.4.flp_ref
  26.4 0.0 collective-permute-done.xp_ref
  26.4 0.0 copy-start
  26.5 0.0 copy-start.1
  26.5 3.0 %shard_map.112 = (f32[2,16,128,128]{3,2,1,0:T(8,128)S(1)}, f32[2,16,64,128]{3,2,1,0:T(8,128)S(1)}, f32[2,16,24,256]{3,2,1,0:T(8,128)S(1)}, f32[8,24,256]{2,1,0:T(8,128)S(1)}, f32[8,128]{1,0:T(8,128)S(1)}) custom-call(f32[2048,256]{1,0:T(8,128)S(1)} %get-tuple-element.27.z_ref, f32[2,8,128,128]{3,2,1,0:T(8,128)S(1)} %collective-permute-done.xp_ref, ...), custom_call_target="tpu_custom_call" | custom-call | flops 2000000000 | bytes 1048576 | tf_op jit(solution)/shard_map/pallas_call | solution.py:698
  29.5 0.0 collective-permute-done.5.sa_ref
  29.5 0.0 collective-permute-done.6.sb_ref
  29.6 1.9 %collective-permute-start.7 = (f32[192,128]{1,0:T(8,128)S(1)}, f32[192,128]{1,0:T(8,128)S(1)}, u32[]{:S(2)}, u32[]{:S(2)}) collective-permute-start(f32[192,128]{1,0:T(8,128)S(1)} %shard_map.113.got_ref), channel_id=1, source_target_pairs={{0,1},{1,0},{2,3},{3,2},{4,5},{5,4},{6,7},{7,6},{8,9},{9,8},{10,11... | collective-permute-start | bytes 294920 | tf_op jit(solution)/shard_map/ppermute | solution.py:716
  31.4 0.3 collective-permute-start.8
  31.7 1.0 %collective-permute-done.8.upp_ref = f32[112,128]{1,0:T(8,128)S(1)} collective-permute-done((f32[112,128]{1,0:T(8,128)S(1)}, f32[112,128]{1,0:T(8,128)S(1)}, u32[]{:S(2)}, u32[]{:S(2)}) %collective-permute-start.8) | collective-permute-done | bytes 57376 | tf_op jit(solution)/shard_map/ppermute | solution.py:716
  32.7 0.0 collective-permute-done.7.gotp_ref
  32.7 0.0 copy-done
  32.7 4.1 %shard_map.114 = f32[2,8,128,128]{3,2,1,0:T(8,128)} custom-call(f32[2,16,128,128]{3,2,1,0:T(8,128)S(1)} %get-tuple-element.35.wf_ref, f32[2,16,64,128]{3,2,1,0:T(8,128)S(1)} %get-tuple-element.36.wl_ref, f32[2,16,24,256]{3,2,1,0:T(8,128)S(1)} %get-tuple-element.37.lh_ref, f32[8,128,128]{2,1,0:T(8,128)S(1)} %get-tuple-element.38.cf_ref, ...), custom_call_target="tpu_custom_call" | custom-call | flops 1000000000 | bytes 1048576 | tf_op jit(solution)/shard_map/pallas_call | solution.py:698
  (9 shorter events, 0.0 us)
Async XLA Ops:
  0.0 26.4 %collective-permute-start = (f32[2,8,128,128]{3,2,1,0:T(8,128)}, f32[2,8,128,128]{3,2,1,0:T(8,128)S(1)}, u32[]{:S(2)}, u32[]{:S(2)}) collective-permute-start(f32[2,8,128,128]{3,2,1,0:T(8,128)} %x_hbm.1), channel_id=1, source_target_pairs={{0,1},{1,0},{2,3},{3,2},{4,5},{5,4},{6,7},{7,6},{8,9},{9,8},{10,11... | collective-permute-start | bytes 3145736 | tf_op jit(solution)/shard_map/ppermute | solution.py:716
  3.2 14.3 %copy-start.6 = (bf16[1424,128]{1,0:T(8,128)(2,1)S(1)}, bf16[1424,128]{1,0:T(8,128)(2,1)}, u32[]{:S(2)}) copy-start(bf16[1424,128]{1,0:T(8,128)(2,1)} %constant.17.clone.refs_0_) | copy-start | bytes 1093636
  6.5 11.0 %collective-permute-start.1 = (f32[208,128]{1,0:T(8,128)}, f32[208,128]{1,0:T(8,128)S(1)}, u32[]{:S(2)}, u32[]{:S(2)}) collective-permute-start(f32[208,128]{1,0:T(8,128)} %get-tuple-element.28), channel_id=1, source_target_pairs={{0,2},{2,0},{4,6},{6,4},{8,10},{10,8},{12,14},{14,12},{16,18},{18,... | collective-permute-start | bytes 319496 | tf_op jit(solution)/shard_map/ppermute | solution.py:712
  6.6 10.9 %collective-permute-start.2 = (f32[208,128]{1,0:T(8,128)}, f32[208,128]{1,0:T(8,128)S(1)}, u32[]{:S(2)}, u32[]{:S(2)}) collective-permute-start(f32[208,128]{1,0:T(8,128)} %get-tuple-element.29), channel_id=1, source_target_pairs={{0,30},{2,4},{4,2},{6,8},{8,6},{10,12},{12,10},{14,16},{16,14},{18... | collective-permute-start | bytes 319496 | tf_op jit(solution)/shard_map/ppermute | solution.py:712
  12.1 1.2 %copy-start.2 = (f32[2,8,128,128]{3,2,1,0:T(8,128)S(1)}, f32[2,8,128,128]{3,2,1,0:T(8,128)}, u32[]{:S(2)}) copy-start(f32[2,8,128,128]{3,2,1,0:T(8,128)} %get-tuple-element.25.x_ref) | copy-start | bytes 3145732
  13.3 1.0 %copy-start.3 = (f32[8,128,128]{2,1,0:T(8,128)S(1)}, f32[8,128,128]{2,1,0:T(8,128)}, u32[]{:S(2)}) copy-start(f32[8,128,128]{2,1,0:T(8,128)} %get-tuple-element.26.clim_ref) | copy-start | bytes 1572868
  14.4 1.1 %copy-start.5 = (bf16[2688,128]{1,0:T(8,128)(2,1)S(1)}, bf16[2688,128]{1,0:T(8,128)(2,1)}, u32[]{:S(2)}) copy-start(bf16[2688,128]{1,0:T(8,128)(2,1)} %constant.15.clone.refs_0_) | copy-start | bytes 2064388
  15.5 2.0 %copy-start.4 = (f32[160,128]{1,0:T(8,128)S(1)}, f32[160,128]{1,0:T(8,128)}, u32[]{:S(2)}) copy-start(f32[160,128]{1,0:T(8,128)} %get-tuple-element.30.sx_ref) | copy-start | bytes 245764
  17.5 9.0 %copy-start.7 = (bf16[1008,128]{1,0:T(8,128)(2,1)S(1)}, bf16[1008,128]{1,0:T(8,128)(2,1)}, u32[]{:S(2)}) copy-start(bf16[1008,128]{1,0:T(8,128)(2,1)} %constant.18.clone.refs_0_) | copy-start | bytes 774148
  18.5 8.0 %collective-permute-start.4 = (f32[432,128]{1,0:T(8,128)S(1)}, f32[432,128]{1,0:T(8,128)S(1)}, u32[]{:S(2)}, u32[]{:S(2)}) collective-permute-start(f32[432,128]{1,0:T(8,128)S(1)} %get-tuple-element.34.fl_ref), channel_id=1, source_target_pairs={{0,1},{1,0},{2,3},{3,2},{4,5},{5,4},{6,7},{7,6},{8,9},{9,8},{10,11... | collective-permute-start | bytes 663560 | tf_op jit(solution)/shard_map/ppermute | solution.py:716
  19.1 7.3 %collective-permute-start.3 = (f32[160,128]{1,0:T(8,128)S(1)}, f32[160,128]{1,0:T(8,128)S(1)}, u32[]{:S(2)}, u32[]{:S(2)}) collective-permute-start(f32[160,128]{1,0:T(8,128)S(1)} %get-tuple-element.33.fr_ref), channel_id=1, source_target_pairs={{0,1},{1,0},{2,3},{3,2},{4,5},{5,4},{6,7},{7,6},{8,9},{9,8},{10,11... | collective-permute-start | bytes 245768 | tf_op jit(solution)/shard_map/ppermute | solution.py:716
  19.2 10.3 %collective-permute-start.5 = (f32[112,128]{1,0:T(8,128)S(1)}, f32[112,128]{1,0:T(8,128)S(1)}, u32[]{:S(2)}, u32[]{:S(2)}) collective-permute-start(f32[112,128]{1,0:T(8,128)S(1)} %get-tuple-element.41), channel_id=1, source_target_pairs={{0,32},{32,0},{64,96},{96,64},{128,160},{160,128},{192,224},{224,1... | collective-permute-start | bytes 172040 | tf_op jit(solution)/shard_map/ppermute | solution.py:712
  20.4 9.1 %collective-permute-start.6 = (f32[112,128]{1,0:T(8,128)S(1)}, f32[112,128]{1,0:T(8,128)S(1)}, u32[]{:S(2)}, u32[]{:S(2)}) collective-permute-start(f32[112,128]{1,0:T(8,128)S(1)} %get-tuple-element.42), channel_id=1, source_target_pairs={{0,224},{32,64},{64,32},{96,128},{128,96},{160,192},{192,160},{224... | collective-permute-start | bytes 172040 | tf_op jit(solution)/shard_map/ppermute | solution.py:712
  26.4 6.2 %copy-start = (bf16[2400,128]{1,0:T(8,128)(2,1)S(1)}, bf16[2400,128]{1,0:T(8,128)(2,1)}, u32[]{:S(2)}) copy-start(bf16[2400,128]{1,0:T(8,128)(2,1)} %constant.19.clone.refs_0_) | copy-start | bytes 1843204
  26.5 6.2 %copy-start.1 = (f32[560,128]{1,0:T(8,128)S(1)}, f32[560,128]{1,0:T(8,128)}, u32[]{:S(2)}) copy-start(f32[560,128]{1,0:T(8,128)} %constant.20.clone.refs_1_) | copy-start | bytes 860164
  29.6 3.1 %collective-permute-start.7 = (f32[192,128]{1,0:T(8,128)S(1)}, f32[192,128]{1,0:T(8,128)S(1)}, u32[]{:S(2)}, u32[]{:S(2)}) collective-permute-start(f32[192,128]{1,0:T(8,128)S(1)} %shard_map.113.got_ref), channel_id=1, source_target_pairs={{0,1},{1,0},{2,3},{3,2},{4,5},{5,4},{6,7},{7,6},{8,9},{9,8},{10,11... | collective-permute-start | bytes 294920 | tf_op jit(solution)/shard_map/ppermute | solution.py:716
  31.4 1.2 %collective-permute-start.8 = (f32[112,128]{1,0:T(8,128)S(1)}, f32[112,128]{1,0:T(8,128)S(1)}, u32[]{:S(2)}, u32[]{:S(2)}) collective-permute-start(f32[112,128]{1,0:T(8,128)S(1)} %get-tuple-element.44.up_ref), channel_id=1, source_target_pairs={{0,1},{1,0},{2,3},{3,2},{4,5},{5,4},{6,7},{7,6},{8,9},{9,8},{10,11... | collective-permute-start | bytes 172040 | tf_op jit(solution)/shard_map/ppermute | solution.py:716

commit v2 on v1

--- a/solution.py
+++ b/solution.py
@@ -244,11 +244,6 @@
     mask("mf", np.concatenate([upper, c["m0"][64:]]))
     mask("ml", c["m1"][64:])
     parts("e_tn", pad_rows(c["E"], 32), 0)
-    ey = np.zeros((128, N))
-    ey[4:8] = c["E"][0:4]
-    for l in range(1, LEVELS):
-        ey[8 * l : 8 * l + 4] = c["E"][4 * l : 4 * l + 4]
-    parts("o", np.concatenate([c["A"].T, ey.T], 1), 1)
     plain("cup", c["cup"])
     plain("cdn", c["cdn"])
     plain("hup", np.tile(c["hup"][:, :, :EXT], (1, 1, IMAGES)))
@@ -283,7 +278,7 @@
 
 @functools.cache
 def packed(names):
-    narrow, wide, places = [np.zeros((16, N))], [np.zeros((16, N))], {}
+    narrow, wide, places = [np.zeros((0, N))], [np.zeros((0, N))], {}
     for name in names:
         kind, axis, array = constants()[name]
         into = wide if kind == "plain" else narrow
@@ -294,7 +289,9 @@
             into += [high.reshape(-1, N), (blocks - high).reshape(-1, N)]
         else:
             into.append(blocks.reshape(-1, N))
-    arrays = [np.concatenate(narrow).astype(ml_dtypes.bfloat16), np.concatenate(wide).astype(np.float32)]
+    arrays = [np.concatenate(narrow).astype(ml_dtypes.bfloat16)]
+    if len(wide) > 1:
+        arrays.append(np.concatenate(wide).astype(np.float32))
     return arrays, places
 
 
@@ -391,11 +388,11 @@
 def first_kernel(x_hbm, clim_hbm, q_hbm, a_ref, b_ref, s_ref, x_ref, clim_ref, q_ref, sems):
     even = even_place("tx")
     ens = lax.axis_index("ens")
-    pairs = [(q_hbm, q_ref)]
+    pairs = [(q_hbm.at[pl.ds(0, q_ref.shape[0])], q_ref)]
     for m in range(2):
         for h in range(2):
             pairs.append((x_hbm.at[m, pl.ds(4 * h, 4)], x_ref.at[m, pl.ds(4 * h, 4)]))
-    pairs.append((clim_hbm, clim_ref))
+    pairs.append((clim_hbm.at[pl.ds(4 * ens, 4)], clim_ref))
     copies = [pltpu.make_async_copy(src, dst, sems.at[i]) for i, (src, dst) in enumerate(pairs)]
     for copy in copies:
         copy.start()
@@ -410,7 +407,7 @@
         right += [lanes(u, i)[0:10] for i in range(4)]
         left += [lanes(u, i)[16:26] for i in range(4)]
     copies[5].wait()
-    d = nt(k("d_nt"), data2(clim_ref[pl.ds(4 * ens, 4)].reshape(4 * N, N), 1))
+    d = nt(k("d_nt"), data2(clim_ref[...].reshape(4 * N, N), 1))
     right += [lanes(d, j)[0:12] for j in range(4)]
     left = jnp.concatenate(left, 0)
     s_ref[...] = left
@@ -419,16 +416,20 @@
     b_ref[...] = jnp.where(even, left, right)
 
 
+def order_kernel(x_ref, out_ref):
+    out_ref[...] = x_ref[0:8]
+
+
 BESIDE = (
     "at", "fold", "foldx", "gst", "kdb", "kz", "mf", "ml", "own", "p0", "p1", "pt", "py", "pyc_nt",
     "y_nt",
 )
 
 
-def beside_kernel(x_ref, clim_ref, *refs):
-    n = 2
+def beside_kernel(x_ref, xp_ref, clim_ref, order_ref, *refs):
+    n = len(packed(BESIDE)[0])
     k = reader(BESIDE, refs[:n])
-    z_ref, s_ref, c_ref, cf_ref, cl_ref = refs[n:]
+    z_ref, zp_ref, s_ref, c_ref, cf_ref, cl_ref = refs[n:]
     ens = lax.axis_index("ens")
     at = k("at")
     for g in range(4):
@@ -442,6 +443,9 @@
             for l in range(4):
                 strip = strip + k("fold", l) * y[40 * i + 8 * l + 8 : 40 * i + 8 * l + 16, N:]
             s_ref[8 * (4 * g + i) : 8 * (4 * g + i) + 8, :] = strip
+    for g in range(4):
+        x = xp_ref[g // 2, 4 * (g % 2) : 4 * (g % 2) + 4].reshape(4 * N, N)
+        zp_ref[4 * N * g : 4 * N * (g + 1), :] = nn(data3(x, 1), at)
     clim = clim_ref[pl.ds(4 * ens, 4)].reshape(4 * N, N)
     y = nn(k("py"), data2(side_by_side(clim), 0))
     y = jnp.concatenate([lanes(y, i)[0:40] for i in range(4)], 0)
@@ -469,14 +473,14 @@
 
 
 def second_kernel(ra_ref, rb_ref, sx_ref, s_ref, c_ref, *refs):
-    n = 2
+    n = len(packed(SECOND)[0])
     k = reader(SECOND, refs[:n])
-    a_ref, b_ref, up_ref, right_ref, left_ref = refs[n:]
+    a_ref, b_ref, share_ref = refs[n:]
     kz = k("kz")
     even, even_y = even_place("tx"), even_place("ty")
     ra, rb = ra_ref[...], rb_ref[...]
     from_right, from_left = jnp.where(even, ra[:160], rb[:160]), jnp.where(even, rb, ra)
-    right_ref[...] = from_right
+    share_ref[432:592] = from_right
     strips = []
     for g in range(2):
         f = taller(from_right[80 * g : 80 * g + 80], 128)
@@ -493,9 +497,9 @@
             strips.append(strip)
     for g in range(4):
         f = jnp.concatenate([from_left[40 * g : 40 * g + 40], sx_ref[40 * g : 40 * g + 40]], 0)
-        left_ref[96 * g : 96 * g + 96] = nn(kz, data3(taller(f, 128), 0))
-    left_ref[384:432] = from_left[160:208]
-    hy = nt(k("y_nt"), data3(left_ref[0:384], 1))
+        share_ref[96 * g : 96 * g + 96] = nn(kz, data3(taller(f, 128), 0))
+    share_ref[384:432] = from_left[160:208]
+    hy = nt(k("y_nt"), data3(share_ref[0:384], 1))
     corner = sum(k("foldx", l) * hy[8 * l : 8 * l + 8] for l in range(LEVELS))
     cx = nt(k("pyc_nt"), data2(taller(from_left[160:208], 128), 1))[0:40]
     cc = nn(data2(cx, 1), k("kdb"))
@@ -505,7 +509,7 @@
     up, down = jnp.concatenate(up, 0), jnp.concatenate(down, 0)
     a_ref[...] = jnp.where(even_y, down, up)
     b_ref[...] = jnp.where(even_y, up, down)
-    up_ref[...] = up
+    share_ref[592:704] = up
 
 
 def filtered(ref, count):
@@ -520,52 +524,52 @@
 )
 
 
-def third_kernel(z_ref, xp_ref, fr_ref, fl_ref, frp_ref, flp_ref, *refs):
-    n = 2
+def third_kernel(z_ref, zp_ref, share_ref, sharep_ref, *refs):
+    n = len(packed(THIRD)[0])
     k = reader(THIRD, refs[:n])
     wf_ref, wl_ref, lh_ref, clh_ref, order_ref = refs[n : n + 5]
     z0_buf, z1_buf, a_buf, b_buf, c_buf, d_buf = refs[n + 5 :]
     first = lax.axis_index("ens") == 0
     inside = lax.broadcasted_iota(jnp.int32, (HALF, N), 1) < HALF
     at = k("at")
-    for side, (fr, fl) in enumerate(((fr_ref, fl_ref), (frp_ref, flp_ref))):
-        for g in range(4):
-            where = 40 * g
-            f = jnp.concatenate([fr[where + 10 * i : where + 10 * i + 5] for i in range(4)], 1)
-            z = tn(data3(taller(f, 16), 0), k("gs"))
-            if side == 0:
-                z = z + z_ref[4 * N * g : 4 * N * (g + 1), :]
-            else:
-                x = xp_ref[g // 2, 4 * (g % 2) : 4 * (g % 2) + 4].reshape(4 * N, N)
-                z = z + nn(data3(x, 1), at)
-            zl = fl[96 * g : 96 * g + 96]
-            lh_ref[side, 4 * g : 4 * g + 4] = nn(data3(zl, 1), at).reshape(4, EXT, 256)
-            for i in range(4):
-                image = 4 * g + i
-                slot = 16 * side + image
-                z0_buf[slot, 0:N] = rows(z, i)[:, :N]
-                z1_buf[slot, 0:N] = rows(z, i)[:, N:]
-                z0_buf[slot, N : N + 8] = zeros(8, N)
-                z1_buf[slot, N : N + 8] = zeros(8, N)
-                low0, high0 = filtered(z0_buf.at[slot], 64)
-                a_buf[slot, 0:64] = filtered(z1_buf.at[slot], 64)[0]
-                a_buf[slot, 64:72] = zeros(8, N)
-                low1, high1 = filtered(a_buf.at[slot], 32)
-                b_buf[slot, 0:32] = low1
-                b_buf[slot, 32:40] = zeros(8, N)
-                low2, high2 = filtered(b_buf.at[slot], 16)
-                c_buf[slot, 0:16] = low2
-                c_buf[slot, 16:24] = zeros(8, N)
-                low3, high3 = filtered(c_buf.at[slot], 8)
-                d_buf[slot, 0:8] = low3
-                d_buf[slot, 8:16] = zeros(8, N)
-                low4, high4 = filtered(d_buf.at[slot], 4)
-                wf_ref[side, image, 0:64] = jnp.where(inside, jnp.concatenate([low1, high1], 0), low0)
-                wf_ref[side, image, 64:128] = high0
-                wl_ref[side, image] = jnp.concatenate(
-                    [low2, high2, low3, high3, zeros(4, N), low4, zeros(4, N), high4], 0
-                )
-    mine, other = fl_ref[384:432], flp_ref[384:432]
+    def group(g, side, z_from, share):
+        f = [share[pl.ds(432 + 40 * g + 8 * i, 8), :] for i in range(5)]
+        f = jnp.concatenate(f, 0)
+        f = jnp.concatenate([f[10 * i : 10 * i + 5] for i in range(4)], 1)
+        z = tn(data3(taller(f, 16), 0), k("gs"))
+        z = z + z_from[pl.ds(4 * N * g, 4 * N), :]
+        zl = share[pl.ds(96 * g, 96), :]
+        lh_ref[side, pl.ds(4 * g, 4)] = nn(data3(zl, 1), at).reshape(4, EXT, 256)
+        for i in range(4):
+            image = 4 * g + i
+            slot = 16 * side + image
+            z0_buf[slot, 0:N] = rows(z, i)[:, :N]
+            z1_buf[slot, 0:N] = rows(z, i)[:, N:]
+            z0_buf[slot, N : N + 8] = zeros(8, N)
+            z1_buf[slot, N : N + 8] = zeros(8, N)
+            low0, high0 = filtered(z0_buf.at[slot], 64)
+            a_buf[slot, 0:64] = filtered(z1_buf.at[slot], 64)[0]
+            a_buf[slot, 64:72] = zeros(8, N)
+            low1, high1 = filtered(a_buf.at[slot], 32)
+            b_buf[slot, 0:32] = low1
+            b_buf[slot, 32:40] = zeros(8, N)
+            low2, high2 = filtered(b_buf.at[slot], 16)
+            c_buf[slot, 0:16] = low2
+            c_buf[slot, 16:24] = zeros(8, N)
+            low3, high3 = filtered(c_buf.at[slot], 8)
+            d_buf[slot, 0:8] = low3
+            d_buf[slot, 8:16] = zeros(8, N)
+            low4, high4 = filtered(d_buf.at[slot], 4)
+            wf_ref[side, image, 0:64] = jnp.where(inside, jnp.concatenate([low1, high1], 0), low0)
+            wf_ref[side, image, 64:128] = high0
+            wl_ref[side, image] = jnp.concatenate(
+                [low2, high2, low3, high3, zeros(4, N), low4, zeros(4, N), high4], 0
+            )
+
+    for g in range(4):
+        group(g, 0, z_ref, share_ref)
+        group(g, 1, zp_ref, sharep_ref)
+    mine, other = share_ref[384:432], sharep_ref[384:432]
     halos = [jnp.where(first, mine, other), jnp.where(first, other, mine)]
     for g in range(2):
         cl = nn(k("kd"), data2(taller(halos[g], 128), 0))
@@ -583,19 +587,20 @@
 
 
 FOURTH = (
-    "cdn", "cl", "cup", "e_tn", "gkc", "gkt", "hdn", "hup", "mch", "mf", "ml", "mlh", "mth", "o",
-    "s0", "s1", "st", "tl",
+    "cdn", "cl", "cup", "e_tn", "gkc", "gkt", "hdn", "hup", "mch", "mf", "ml", "mlh", "mth", "s0",
+    "s1", "st", "tl",
 )
 
 
-def fourth_kernel(wf_ref, wl_ref, lh_ref, cf_ref, cl_ref, clh_ref, got_ref, gotp_ref, up_ref, upp_ref, *refs):
-    n = 2
+def fourth_kernel(wf_ref, wl_ref, lh_ref, cf_ref, cl_ref, clh_ref, got_ref, gotp_ref, share_ref, sharep_ref, *refs):
+    n = len(packed(FOURTH)[0])
     k = reader(FOURTH, refs[:n])
-    out_ref = refs[n]
+    out_hbm, out_ref, sems, *bufs = refs[n:]
+    copies = []
     first = lax.axis_index("ens") == 0
     belows, aboves, ups, lhs, chs = [], [], [], [], []
-    for got, up in ((got_ref, up_ref), (gotp_ref, upp_ref)):
-        below, above, up = got[0:80], got[80:192], up[...]
+    for got, share in ((got_ref, share_ref), (gotp_ref, sharep_ref)):
+        below, above, up = got[0:80], got[80:192], share[592:704]
         hb = jnp.concatenate([below[64 + 4 * g : 68 + 4 * g] for g in range(3)], 1)
         lhs.append(tn(data3(taller(hb, 16), 0), k("gkt")))
         hu = jnp.concatenate([up[64 + 4 * g : 68 + 4 * g] for g in range(3)], 1)
@@ -675,34 +680,66 @@
         top0 = jnp.concatenate([k("tl", 0) * sth[i] for i in range(4)], 0)
         top1 = jnp.concatenate([k("tl", l) * sth[i] for l in range(1, LEVELS) for i in range(4)], 0)
         tu = jnp.concatenate([nn(data3(top0, 1), k("s0")), nn(data3(top1, 1), k("s1"))], 0)
-        full = []
         for i in range(4):
+            m, v = i // 2, 2 * g + i % 2
+            image = 8 * m + v
             r = tn(data3(taller(slh[i], 32), 0), k("e_tn"))
             at = HALF * i
-            parts = [upper[at : at + HALF, :N], lower[at : at + HALF], upper[at : at + HALF, N:], rest[at : at + HALF]]
-            t = []
-            for l in range(LEVELS):
-                edge = 128 * l + 8 * (8 * (i // 2) + 2 * g + i % 2)
-                t.append(tu[8 * (4 * l + i) : 8 * (4 * l + i) + 8] + tu_edge[edge : edge + 8])
-            t.append(zeros(88, N))
-            full.append(jnp.concatenate([jnp.concatenate(parts, 0) + r] + t, 0))
-        out = nn(k("o"), data3(jnp.concatenate(full, 1), 0))
-        for i in range(4):
-            out_ref[i // 2, 2 * g + i % 2] = lanes(out, i)
+            one = upper[at : at + HALF, N:] + r[N : N + HALF]
+            more = rest[at : at + HALF] + r[N + HALF :]
+            bands = [
+                (upper[at : at + HALF, :N] + r[:HALF], lower[at : at + HALF] + r[HALF:N]),
+                (one[0:32], one[32:64]),
+                (more[0:16], more[16:32]),
+                (more[32:40], more[40:48]),
+                (more[52:56], more[60:64]),
+            ]
+            for l, (low, high) in enumerate(bands):
+                at = 128 * l + 8 * image
+                t = tu[8 * (4 * l + i) : 8 * (4 * l + i) + 8] + tu_edge[at : at + 8]
+                t = t[4:8] if l == 0 else t[0:4]
+                buf = bufs[l]
+                buf[2 * image, 14:16] = t[0:2]
+                buf[2 * image + 1, 14:16] = t[2:4]
+                buf[2 * image, 16 : 16 + low.shape[0]] = low
+                buf[2 * image + 1, 16 : 16 + low.shape[0]] = high
+            for l in reversed(range(LEVELS)):
+                count = HALF >> l
+                first_row = 16 if l == 0 else 8
+                size = 16 + count - first_row
+                here = [bufs[l][2 * image + b, first_row : first_row + size] for b in range(2)]
+                prior = [bufs[l][2 * image + b, first_row - 1 : first_row - 1 + size] for b in range(2)]
+                pair = [
+                    H[j] * here[0] + G[j] * here[1] + H[j + 2] * prior[0] + G[j + 2] * prior[1] for j in range(2)
+                ]
+                for j in range(2):
+                    if l == 0:
+                        out_ref[m, v, pl.ds(j, size, stride=2), :] = pair[j]
+                    else:
+                        place = pl.ds(j, size, stride=2)
+                        bufs[l - 1][2 * image, place, :] = bufs[l - 1][2 * image, place, :] + pair[j]
+        for m in range(2):
+            part = pl.ds(2 * g, 2)
+            copy = pltpu.make_async_copy(out_ref.at[m, part], out_hbm.at[m, part], sems.at[2 * g + m])
+            copy.start()
+            copies.append(copy)
+    for copy in copies:
+        copy.wait()
 
 
 VMEM = pl.BlockSpec(memory_space=pltpu.VMEM)
-
-
-def call(kernel, arguments, shapes, flops, scratch=(), in_specs=None, limit=40):
+HBM = pl.BlockSpec(memory_space=pltpu.HBM)
+
+
+def call(kernel, arguments, shapes, flops, scratch=(), in_specs=None, limit=40, out_specs=None):
     return pl.pallas_call(
         kernel,
         in_specs=in_specs or [VMEM] * len(arguments),
-        out_specs=[VMEM] * len(shapes),
+        out_specs=out_specs or [VMEM] * len(shapes),
         out_shape=[s if hasattr(s, "dtype") else jax.ShapeDtypeStruct(s, jnp.float32) for s in shapes],
         scratch_shapes=scratch,
         cost_estimate=pl.CostEstimate(flops=flops, bytes_accessed=1 << 20, transcendentals=0),
-        compiler_params=pltpu.CompilerParams(vmem_limit_bytes=limit * 1024 * 1024),
+        compiler_params=pltpu.CompilerParams(vmem_limit_bytes=int(limit * 1024 * 1024)),
     )(*arguments)
 
 
@@ -720,47 +757,45 @@
     return pltpu.VMEM((count, height, N), jnp.float32)
 
 
+PAD = True
+
+
 def held(names):
     return [jnp.asarray(array) for array in packed(names)[0]]
 
 
-def shards(x_hbm, clim_hbm):
-    xp = partner(x_hbm)
+def shards(x, clim):
+    xp = partner(x)
     m1, m2 = (X_ROWS, N), (Y_ROWS, N)
     q = held(FIRST)[0]
-    hbm = pl.BlockSpec(memory_space=pltpu.HBM)
-    xa, xb, sx, x, clim = call(
-        first_kernel,
-        (x_hbm, clim_hbm, q),
-        [m1, m1, (160, N), x_hbm.shape, clim_hbm.shape],
-        10**8,
-        [pltpu.VMEM(q.shape, q.dtype), pltpu.SemaphoreType.DMA((6,))],
-        [hbm] * 3,
-        60,
-    )
+    padded = jnp.concatenate([q, jnp.zeros((4096 - q.shape[0], N), q.dtype)], 0) if PAD else q
+    scratch = [pltpu.VMEM(x.shape, x.dtype), pltpu.VMEM((4, N, N), x.dtype)]
+    scratch += [pltpu.VMEM(q.shape, q.dtype), pltpu.SemaphoreType.DMA((6,))]
+    xa, xb, sx = call(first_kernel, (x, clim, padded), [m1, m1, (160, N)], 10**8, scratch, [HBM] * 3, 53.6)
     ra, rb = exchange(xa, "tx", 0), exchange(xb, "tx", 1)
-    z, strips, tops, cf, cl = call(
+    order = call(order_kernel, (sx,), [(8, N)], 10**6)[0]
+    z, zp, strips, tops, cf, cl = call(
         beside_kernel,
-        (x, clim, *held(BESIDE)),
-        [(IMAGES * N, 256), (IMAGES * 8, N), (32, N), (8, N, N), (8, HALF, N)],
+        (x, xp, clim, order, *held(BESIDE)),
+        [(IMAGES * N, 256), (IMAGES * N, 256), (IMAGES * 8, N), (32, N), (8, N, N), (8, HALF, N)],
         10**9,
     )
-    ya, yb, up, fr, fl = call(
-        second_kernel, (ra, rb, sx, strips, tops, *held(SECOND)), [m2, m2, m2, (160, N), (432, N)], 10**9
-    )
+    ya, yb, share = call(second_kernel, (ra, rb, sx, strips, tops, *held(SECOND)), [m2, m2, (704, N)], 10**9)
     sa, sb = exchange(ya, "ty", 0), exchange(yb, "ty", 1)
-    frp, flp, upp = partner(fr), partner(fl), partner(up)
+    sharep = partner(share)
     wf, wl, lh, clh, order = call(
         third_kernel,
-        (z, xp, fr, fl, frp, flp, *held(THIRD)),
+        (z, zp, share, sharep, *held(THIRD)),
         [(2, IMAGES, N, N), (2, IMAGES, HALF, N), (2, IMAGES, EXT, 256), (8, EXT, 256), (8, N)],
         2 * 10**9,
         [buffer(32, h) for h in (136, 136, 72, 40, 24, 16)],
     )
     got = call(sort_kernel, (sa, sb, order), [(192, N)], 10**6)[0]
     gotp = partner(got)
-    arguments = (wf, wl, lh, cf, cl, clh, got, gotp, up, upp, *held(FOURTH))
-    return call(fourth_kernel, arguments, [x_hbm.shape], 10**9)[0]
+    arguments = (wf, wl, lh, cf, cl, clh, got, gotp, share, sharep, *held(FOURTH))
+    scratch = [pltpu.VMEM(x.shape, x.dtype), pltpu.SemaphoreType.DMA((8,))]
+    scratch += [buffer(32, 16 + (HALF >> l)) for l in range(LEVELS)]
+    return call(fourth_kernel, arguments, [x.shape], 10**9, scratch, out_specs=[HBM])[0]
 
 
 def solution(mesh):

time: 37 us -> 33.7 us (0.911)
  local copies, waits for them, and re-layouts: 3.39 us -> 0.03 us
  Pallas kernels: 13.3 us -> 12 us
  starting transfers between devices: 18.9 us -> 20 us
    unnamed x16 -> x14, local copies, waits for them, and re-layouts: 3.39 us -> 0.03 us
    ppermute x4, starting transfers between devices: 12.8 us -> 14.8 us  [exchange(): return lax.ppermute(value, axis, pairs)]
    pallas_call x6 -> x7, Pallas kernels: 13.3 us -> 12 us  [call(): pl.pallas_call(kernel, in_specs=in_specs or [VMEM] * len(arguments), out_...]
    ppermute x5 -> x3, starting transfers between devices: 6.12 us -> 5.21 us  [partner(): return lax.ppermute(value, 'ens', [(0, 1), (1, 0)])]
    ppermute x5 -> x3, waiting for transfers between devices: 0.97 us -> 0.95 us  [partner(): return lax.ppermute(value, 'ens', [(0, 1), (1, 0)])]
  transfers between devices with their start and end apart: 9 -> 7, of which waited for: 1 -> 2; matrix products, arithmetic and copies ran while one was open for 0% -> 0% of each run, Pallas kernels for 25% -> 22%
where the time goes in v2:
time: 33.7 us; the launch traced here: 33.6 us
  starting transfers between devices  20 us (59%)
  Pallas kernels  12 us (36%)
  waiting for transfers between devices  1.31 us (4%)
    ppermute x4, starting transfers between devices, exchange(): return lax.ppermute(value, axis, pairs)  14.8 us
    pallas_call x7, Pallas kernels, call(): pl.pallas_call(kernel, in_specs=in_specs or [VMEM] * len(arguments), out_...  12 us
    ppermute x3, starting transfers between devices, partner(): return lax.ppermute(value, 'ens', [(0, 1), (1, 0)])  5.21 us
    ppermute x3, waiting for transfers between devices, partner(): return lax.ppermute(value, 'ens', [(0, 1), (1, 0)])  0.95 us
  transfers between devices with their start and end apart: 7, of which 2 were waited for; matrix products, arithmetic and copies ran while one was open for 0% of the time, Pallas kernels for 22%

profile of v2, /device:TPU:1, one launch (start us, length us, event | category | flops | bytes accessed | tf_op | source)
XLA Modules:
  0.0 33.6 jit_solution(3273441412988933961)
XLA Ops:
  0.0 0.0 copy-start.4
  0.0 0.0 copy-start
  0.0 0.0 copy-start.1
  0.0 3.2 %collective-permute-start = (f32[2,8,128,128]{3,2,1,0:T(8,128)}, f32[2,8,128,128]{3,2,1,0:T(8,128)S(1)}, u32[]{:S(2)}, u32[]{:S(2)}) collective-permute-start(f32[2,8,128,128]{3,2,1,0:T(8,128)} %x_ref.1), channel_id=1, source_target_pairs={{0,1},{1,0},{2,3},{3,2},{4,5},{5,4},{6,7},{7,6},{8,9},{9,8},{10,11... | collective-permute-start | bytes 3145736 | tf_op jit(solution)/shard_map/ppermute | solution.py:753
  3.2 2.2 %shard_map.82 = (f32[208,128]{1,0:T(8,128)S(1)}, f32[208,128]{1,0:T(8,128)S(1)}, f32[160,128]{1,0:T(8,128)S(1)}) custom-call(f32[2,8,128,128]{3,2,1,0:T(8,128)} %x_ref.1, f32[8,128,128]{2,1,0:T(8,128)} %clim_ref.1, bf16[4096,128]{1,0:T(8,128)(2,1)} %constant.22.q_hbm), custom_call_target="tpu_custom_call" | custom-call | flops 100000000 | bytes 1048576 | tf_op jit(solution)/shard_map/pallas_call | solution.py:735
  5.4 0.0 copy-start.5
  5.4 0.1 collective-permute-start.1
  5.5 5.6 %collective-permute-start.2 = (f32[208,128]{1,0:T(8,128)S(1)}, f32[208,128]{1,0:T(8,128)S(1)}, u32[]{:S(2)}, u32[]{:S(2)}) collective-permute-start(f32[208,128]{1,0:T(8,128)S(1)} %get-tuple-element.26), channel_id=1, source_target_pairs={{0,30},{2,4},{4,2},{6,8},{8,6},{10,12},{12,10},{14,16},{16,14},{18... | collective-permute-start | bytes 319496 | tf_op jit(solution)/shard_map/ppermute | solution.py:749
  11.1 0.0 collective-permute-done.xp_ref
  11.1 0.0 copy-done.4
  11.1 0.0 copy-done
  11.1 0.0 copy-done.1
  11.1 2.5 %shard_map.84 = (f32[2048,256]{1,0:T(8,128)S(1)}, f32[2048,256]{1,0:T(8,128)S(1)}, f32[128,128]{1,0:T(8,128)S(1)}, f32[32,128]{1,0:T(8,128)S(1)}, f32[8,128,128]{2,1,0:T(8,128)S(1)}, /*index=5*/f32[8,64,128]{2,1,0:T(8,128)S(1)}) custom-call(f32[2,8,128,128]{3,2,1,0:T(8,128)S(1)} %copy-done, f32[2,8,128,128]{3,2,1,0:T(8,128)S(1)} %collective-permute-done.xp_ref, ...), custom_call_target="tpu_custom_call" | custom-call | flops 1000000000 | bytes 1048576 | tf_op jit(solution)/shard_map/pallas_call | solution.py:735
  13.7 0.0 copy-start.6
  13.7 0.0 collective-permute-done.1.ra_ref
  13.7 0.4 %collective-permute-done.2.rb_ref = f32[208,128]{1,0:T(8,128)S(1)} collective-permute-done((f32[208,128]{1,0:T(8,128)S(1)}, f32[208,128]{1,0:T(8,128)S(1)}, u32[]{:S(2)}, u32[]{:S(2)}) %collective-permute-start.2) | collective-permute-done | bytes 106528 | tf_op jit(solution)/shard_map/ppermute | solution.py:749
  14.1 0.0 copy-done.5
  14.1 0.9 %shard_map.85 = (f32[112,128]{1,0:T(8,128)S(1)}, f32[112,128]{1,0:T(8,128)S(1)}, f32[704,128]{1,0:T(8,128)S(1)}) custom-call(f32[208,128]{1,0:T(8,128)S(1)} %collective-permute-done.1.ra_ref, f32[208,128]{1,0:T(8,128)S(1)} %collective-permute-done.2.rb_ref, f32[160,128]{1,0:T(8,128)S(1)} %get-tuple-element.22.x_ref.sx_ref, ...), custom_call_target="tpu_custom_call" | custom-call | flops 1000000000 | bytes 1048576 | tf_op jit(solution)/shard_map/pallas_call | solution.py:735
  15.0 1.1 %collective-permute-start.3 = (f32[704,128]{1,0:T(8,128)S(1)}, f32[704,128]{1,0:T(8,128)S(1)}, u32[]{:S(2)}, u32[]{:S(2)}) collective-permute-start(f32[704,128]{1,0:T(8,128)S(1)} %get-tuple-element.29.share_ref), channel_id=1, source_target_pairs={{0,1},{1,0},{2,3},{3,2},{4,5},{5,4},{6,7},{7,6},{8,9},{9,8},{10,11... | collective-permute-start | bytes 1081352 | tf_op jit(solution)/shard_map/ppermute | solution.py:753
  16.1 1.2 %collective-permute-start.4 = (f32[112,128]{1,0:T(8,128)S(1)}, f32[112,128]{1,0:T(8,128)S(1)}, u32[]{:S(2)}, u32[]{:S(2)}) collective-permute-start(f32[112,128]{1,0:T(8,128)S(1)} %get-tuple-element.36), channel_id=1, source_target_pairs={{0,32},{32,0},{64,96},{96,64},{128,160},{160,128},{192,224},{224,1... | collective-permute-start | bytes 172040 | tf_op jit(solution)/shard_map/ppermute | solution.py:749
  17.3 7.8 %collective-permute-start.5 = (f32[112,128]{1,0:T(8,128)S(1)}, f32[112,128]{1,0:T(8,128)S(1)}, u32[]{:S(2)}, u32[]{:S(2)}) collective-permute-start(f32[112,128]{1,0:T(8,128)S(1)} %get-tuple-element.37), channel_id=1, source_target_pairs={{0,224},{32,64},{64,32},{96,128},{128,96},{160,192},{192,160},{224... | collective-permute-start | bytes 172040 | tf_op jit(solution)/shard_map/ppermute | solution.py:749
  25.2 0.0 collective-permute-done.3.sharep_ref
  25.2 0.0 copy-done.6
  25.2 0.0 copy-start.2
  25.2 2.6 %shard_map.86 = (f32[2,16,128,128]{3,2,1,0:T(8,128)S(1)}, f32[2,16,64,128]{3,2,1,0:T(8,128)S(1)}, f32[2,16,24,256]{3,2,1,0:T(8,128)S(1)}, f32[8,24,256]{2,1,0:T(8,128)S(1)}, f32[8,128]{1,0:T(8,128)S(1)}) custom-call(f32[2048,256]{1,0:T(8,128)S(1)} %get-tuple-element.23.z_ref, f32[2048,256]{1,0:T(8,128)S(1)} %get-tuple-element.24.zp_ref, ...), custom_call_target="tpu_custom_call" | custom-call | flops 2000000000 | bytes 1048576 | tf_op jit(solution)/shard_map/pallas_call | solution.py:735
  27.8 0.0 collective-permute-done.4.sa_ref
  27.8 0.0 collective-permute-done.5.sb_ref
  27.8 0.9 %collective-permute-start.6 = (f32[192,128]{1,0:T(8,128)S(1)}, f32[192,128]{1,0:T(8,128)S(1)}, u32[]{:S(2)}, u32[]{:S(2)}) collective-permute-start(f32[192,128]{1,0:T(8,128)S(1)} %shard_map.87.got_ref), channel_id=1, source_target_pairs={{0,1},{1,0},{2,3},{3,2},{4,5},{5,4},{6,7},{7,6},{8,9},{9,8},{10,11... | collective-permute-start | bytes 294920 | tf_op jit(solution)/shard_map/ppermute | solution.py:753
  28.8 0.9 %collective-permute-done.6.gotp_ref = f32[192,128]{1,0:T(8,128)S(1)} collective-permute-done((f32[192,128]{1,0:T(8,128)S(1)}, f32[192,128]{1,0:T(8,128)S(1)}, u32[]{:S(2)}, u32[]{:S(2)}) %collective-permute-start.6) | collective-permute-done | bytes 98336 | tf_op jit(solution)/shard_map/ppermute | solution.py:753
  29.7 0.0 copy-done.2
  29.7 0.0 copy-done.3
  29.7 3.8 %shard_map.88 = f32[2,8,128,128]{3,2,1,0:T(8,128)} custom-call(f32[2,16,128,128]{3,2,1,0:T(8,128)S(1)} %get-tuple-element.30.wf_ref, f32[2,16,64,128]{3,2,1,0:T(8,128)S(1)} %get-tuple-element.31.wl_ref, f32[2,16,24,256]{3,2,1,0:T(8,128)S(1)} %get-tuple-element.32.lh_ref, f32[8,128,128]{2,1,0:T(8,128)S(1)} %get-tuple-element.33.cf_ref, ...), custom_call_target="tpu_custom_call" | custom-call | flops 1000000000 | bytes 1048576 | tf_op jit(solution)/shard_map/pallas_call | solution.py:735
  (3 shorter events, 0.0 us)
Async XLA Ops:
  0.0 11.1 %copy-start.4 = (bf16[2672,128]{1,0:T(8,128)(2,1)S(1)}, bf16[2672,128]{1,0:T(8,128)(2,1)}, u32[]{:S(2)}) copy-start(bf16[2672,128]{1,0:T(8,128)(2,1)} %constant.15.clone.refs_0_) | copy-start | bytes 2052100
  0.0 11.1 %copy-start = (f32[2,8,128,128]{3,2,1,0:T(8,128)S(1)}, f32[2,8,128,128]{3,2,1,0:T(8,128)}, u32[]{:S(2)}) copy-start(f32[2,8,128,128]{3,2,1,0:T(8,128)} %x_ref.1) | copy-start | bytes 3145732
  0.0 11.1 %copy-start.1 = (f32[8,128,128]{2,1,0:T(8,128)S(1)}, f32[8,128,128]{2,1,0:T(8,128)}, u32[]{:S(2)}) copy-start(f32[8,128,128]{2,1,0:T(8,128)} %clim_ref.1) | copy-start | bytes 1572868
  0.0 11.1 %collective-permute-start = (f32[2,8,128,128]{3,2,1,0:T(8,128)}, f32[2,8,128,128]{3,2,1,0:T(8,128)S(1)}, u32[]{:S(2)}, u32[]{:S(2)}) collective-permute-start(f32[2,8,128,128]{3,2,1,0:T(8,128)} %x_ref.1), channel_id=1, source_target_pairs={{0,1},{1,0},{2,3},{3,2},{4,5},{5,4},{6,7},{7,6},{8,9},{9,8},{10,11... | collective-permute-start | bytes 3145736 | tf_op jit(solution)/shard_map/ppermute | solution.py:753
  5.4 8.7 %copy-start.5 = (bf16[1408,128]{1,0:T(8,128)(2,1)S(1)}, bf16[1408,128]{1,0:T(8,128)(2,1)}, u32[]{:S(2)}) copy-start(bf16[1408,128]{1,0:T(8,128)(2,1)} %constant.16.clone.refs_0_) | copy-start | bytes 1081348
  5.4 8.3 %collective-permute-start.1 = (f32[208,128]{1,0:T(8,128)S(1)}, f32[208,128]{1,0:T(8,128)S(1)}, u32[]{:S(2)}, u32[]{:S(2)}) collective-permute-start(f32[208,128]{1,0:T(8,128)S(1)} %get-tuple-element.25), channel_id=1, source_target_pairs={{0,2},{2,0},{4,6},{6,4},{8,10},{10,8},{12,14},{14,12},{16,18},{18,... | collective-permute-start | bytes 319496 | tf_op jit(solution)/shard_map/ppermute | solution.py:749
  5.5 8.6 %collective-permute-start.2 = (f32[208,128]{1,0:T(8,128)S(1)}, f32[208,128]{1,0:T(8,128)S(1)}, u32[]{:S(2)}, u32[]{:S(2)}) collective-permute-start(f32[208,128]{1,0:T(8,128)S(1)} %get-tuple-element.26), channel_id=1, source_target_pairs={{0,30},{2,4},{4,2},{6,8},{8,6},{10,12},{12,10},{14,16},{16,14},{18... | collective-permute-start | bytes 319496 | tf_op jit(solution)/shard_map/ppermute | solution.py:749
  13.7 11.5 %copy-start.6 = (bf16[992,128]{1,0:T(8,128)(2,1)S(1)}, bf16[992,128]{1,0:T(8,128)(2,1)}, u32[]{:S(2)}) copy-start(bf16[992,128]{1,0:T(8,128)(2,1)} %constant.17.clone.refs_0_) | copy-start | bytes 761860
  15.0 10.1 %collective-permute-start.3 = (f32[704,128]{1,0:T(8,128)S(1)}, f32[704,128]{1,0:T(8,128)S(1)}, u32[]{:S(2)}, u32[]{:S(2)}) collective-permute-start(f32[704,128]{1,0:T(8,128)S(1)} %get-tuple-element.29.share_ref), channel_id=1, source_target_pairs={{0,1},{1,0},{2,3},{3,2},{4,5},{5,4},{6,7},{7,6},{8,9},{9,8},{10,11... | collective-permute-start | bytes 1081352 | tf_op jit(solution)/shard_map/ppermute | solution.py:753
  16.1 11.7 %collective-permute-start.4 = (f32[112,128]{1,0:T(8,128)S(1)}, f32[112,128]{1,0:T(8,128)S(1)}, u32[]{:S(2)}, u32[]{:S(2)}) collective-permute-start(f32[112,128]{1,0:T(8,128)S(1)} %get-tuple-element.36), channel_id=1, source_target_pairs={{0,32},{32,0},{64,96},{96,64},{128,160},{160,128},{192,224},{224,1... | collective-permute-start | bytes 172040 | tf_op jit(solution)/shard_map/ppermute | solution.py:749
  17.3 10.5 %collective-permute-start.5 = (f32[112,128]{1,0:T(8,128)S(1)}, f32[112,128]{1,0:T(8,128)S(1)}, u32[]{:S(2)}, u32[]{:S(2)}) collective-permute-start(f32[112,128]{1,0:T(8,128)S(1)} %get-tuple-element.37), channel_id=1, source_target_pairs={{0,224},{32,64},{64,32},{96,128},{128,96},{160,192},{192,160},{224... | collective-permute-start | bytes 172040 | tf_op jit(solution)/shard_map/ppermute | solution.py:749
  25.2 4.5 %copy-start.2 = (bf16[1616,128]{1,0:T(8,128)(2,1)S(1)}, bf16[1616,128]{1,0:T(8,128)(2,1)}, u32[]{:S(2)}) copy-start(bf16[1616,128]{1,0:T(8,128)(2,1)} %constant.18.clone.refs_0_) | copy-start | bytes 1241092
  25.2 4.5 %copy-start.3 = (f32[544,128]{1,0:T(8,128)S(1)}, f32[544,128]{1,0:T(8,128)}, u32[]{:S(2)}) copy-start(f32[544,128]{1,0:T(8,128)} %constant.19.clone.refs_1_) | copy-start | bytes 835588
  27.8 1.9 %collective-permute-start.6 = (f32[192,128]{1,0:T(8,128)S(1)}, f32[192,128]{1,0:T(8,128)S(1)}, u32[]{:S(2)}, u32[]{:S(2)}) collective-permute-start(f32[192,128]{1,0:T(8,128)S(1)} %shard_map.87.got_ref), channel_id=1, source_target_pairs={{0,1},{1,0},{2,3},{3,2},{4,5},{5,4},{6,7},{7,6},{8,9},{9,8},{10,11... | collective-permute-start | bytes 294920 | tf_op jit(solution)/shard_map/ppermute | solution.py:753
